TPU v7x, 32 devices: a whole 2x2x4 slice. The times are simulated.
32 devices in a mesh: dp: 4 (over z), ctx: 8 (over y, x, core).
Axes of the slice: x: 2, y: 2, z: 4, core: 2. Of those that a mesh axis runs over, the one named last changes fastest.
Arguments:
- hidden: bfloat16 [4, 2048, 8192], P('dp', 'ctx'), may hold values from -6 to 6
- queries: bfloat16 [4, 2048, 4096], P('dp', 'ctx')
- layout: int32 [4, 16], P('dp'), may hold values from 0 to 15, each once within a row
- boundary: int32 [4], P('dp'), may hold values from 1 to 2047
- key_matrix: bfloat16 [8192, 512], P(('dp', 'ctx')), may hold values from -0.0625 to 0.0625
- value_matrix: bfloat16 [8192, 512], P(('dp', 'ctx')), may hold values from -0.0625 to 0.0625
Outputs:
- attended: bfloat16 [4, 2048, 4096], P('dp', 'ctx')
Inputs may be any that keep to these rules, and one draw needn't show every extreme that they name: Each row holds every block number of 0 to 15 once; local block b of ctx index c is layout[2 c + b].
All inputs are finite; a program needn't handle non-finite values.
Results may differ from a plain program's by a relative error of at most 0.011.
Values may be sent and summed in bfloat16 or wider, within the bound.
No kernel may reach another device: no remote copies, remote signals or barrier semaphores. Data moves between devices by JAX's collectives and lax.ppermute only.
A program may use at most 320 MiB of HBM per device.

v0:
```python
import functools

import jax
import jax.numpy as jnp
from jax import lax
from jax.experimental import pallas as pl
from jax.experimental.pallas import tpu as pltpu
from jax.sharding import PartitionSpec as P

HEAD_WIDTH = 128
LOG2_E = 1.4426950408889634
ARRANGE_LIMIT = 12 * 2**20
PROJECT_LIMIT = 18 * 2**20
ATTEND_LIMIT = 14 * 2**20


def swapped(value, mask):
    size = lax.axis_size("ctx")
    return lax.ppermute(value, "ctx", [(i, i ^ mask) for i in range(size)])


def across(value, mask):
    size = lax.axis_size("dp")
    return lax.ppermute(value, "dp", [(i, i ^ mask) for i in range(size)])


def arrange_kernel(blocks, starts, own_ref, other_ref, out_ref, sems):
    core = starts[0]
    rows = own_ref.shape[0]
    depth = own_ref.shape[1] // blocks
    copies = []
    for source, place in ((own_ref, core), (other_ref, 1 - core)):
        for index in range(blocks):
            first = pl.multiple_of(starts[1 + index] * depth, depth)
            copies.append(
                pltpu.make_async_copy(
                    source.at[:, pl.ds(first, depth)],
                    out_ref.at[pl.ds(pl.multiple_of(place * rows, rows), rows), pl.ds(index * depth, depth)],
                    sems.at[len(copies)],
                )
            )
    for copy in copies:
        copy.start()
    for copy in copies:
        copy.wait()


def arrange(starts, own, other):
    blocks = starts.shape[0] - 1
    rows, columns = own.shape
    anywhere = pl.BlockSpec(memory_space=pl.ANY)
    return pl.pallas_call(
        functools.partial(arrange_kernel, blocks),
        out_shape=jax.ShapeDtypeStruct((2 * rows, columns), own.dtype),
        in_specs=[pl.BlockSpec(memory_space=pltpu.SMEM), anywhere, anywhere],
        out_specs=pl.BlockSpec(memory_space=pltpu.VMEM),
        scratch_shapes=[pltpu.SemaphoreType.DMA((2 * blocks,))],
        compiler_params=pltpu.CompilerParams(vmem_limit_bytes=ARRANGE_LIMIT),
        cost_estimate=pl.CostEstimate(flops=0, bytes_accessed=8 * rows * columns, transcendentals=0),
        name="arrange",
    )(starts, own, other)


def project_kernel(first, column, has_total, tokens, *refs):
    pieces, out_ref = refs[: -1 - has_total], refs[-1]
    width = out_ref.shape[1]
    total = refs[-2][:, column : column + width] if has_total else None
    for piece in pieces:
        depth = piece.shape[0]
        part = jnp.dot(tokens[:, first : first + depth], piece[...], preferred_element_type=jnp.float32)
        total = part if total is None else total + part
        first += depth
    out_ref[...] = total.astype(out_ref.dtype)


def project(tokens, first, pieces, total, column, dtype):
    rows, width = tokens.shape[0], pieces[0].shape[1]
    vmem = pl.BlockSpec(memory_space=pltpu.VMEM)
    depth = sum(piece.shape[0] for piece in pieces)
    totals = [] if total is None else [total]
    return pl.pallas_call(
        functools.partial(project_kernel, first, column, len(totals)),
        out_shape=jax.ShapeDtypeStruct((rows, width), dtype),
        in_specs=[vmem] * (1 + len(pieces) + len(totals)),
        out_specs=vmem,
        compiler_params=pltpu.CompilerParams(vmem_limit_bytes=PROJECT_LIMIT),
        cost_estimate=pl.CostEstimate(flops=2 * rows * depth * width, bytes_accessed=2 * rows * depth, transcendentals=0),
        name="project",
    )(tokens, *pieces, *totals)


def attend_kernel(scale, group, core, bias, queries, held, sent, *refs):
    out_ref, key_rows, value_rows = refs[-3:]
    is_keys = core[0] == 0
    key_rows[...] = jnp.where(is_keys, held[...], sent[...])
    value_rows[:, :HEAD_WIDTH] = jnp.where(is_keys, sent[...], held[...])
    value_rows[:, HEAD_WIDTH:] = jnp.ones((value_rows.shape[0], HEAD_WIDTH), jnp.bfloat16)
    step = 128
    for head in range(group):
        columns = slice(head * HEAD_WIDTH, (head + 1) * HEAD_WIDTH)
        for row in range(0, queries.shape[0], step):
            scores = lax.dot_general(
                queries[row : row + step, columns],
                key_rows[...],
                (((1,), (1,)), ((), ())),
                preferred_element_type=jnp.float32,
            )
            scores = scores * scale + bias[row : row + step, :]
            peak = jnp.max(scores, axis=1, keepdims=True)
            probs = jnp.exp2(scores - peak).astype(jnp.bfloat16)
            summed = jnp.dot(probs, value_rows[...], preferred_element_type=jnp.float32)
            out_ref[row : row + step, columns] = (summed[:, :HEAD_WIDTH] / summed[:, HEAD_WIDTH:]).astype(out_ref.dtype)


def attend(core, bias, queries, sides, before, first, head, kv_heads):
    rows, width = queries.shape
    block = width // kv_heads
    count = bias.shape[1]
    vmem = pl.BlockSpec(memory_space=pltpu.VMEM)
    chosen = pl.BlockSpec((rows, block), lambda i: (0, first + head))
    side = pl.BlockSpec((count, HEAD_WIDTH), lambda i: (0, head))
    in_specs = [pl.BlockSpec(memory_space=pltpu.SMEM), vmem, chosen, side, side]
    operands = [core, bias, queries, *sides]
    aliases = {}
    if before is not None:
        aliases = {len(operands): 0}
        in_specs.append(pl.BlockSpec(memory_space=pl.ANY))
        operands.append(before)
    return pl.pallas_call(
        functools.partial(attend_kernel, HEAD_WIDTH**-0.5 * LOG2_E, block // HEAD_WIDTH),
        grid=(1,),
        out_shape=jax.ShapeDtypeStruct((rows, width), jnp.bfloat16),
        in_specs=in_specs,
        out_specs=chosen,
        input_output_aliases=aliases,
        scratch_shapes=[
            pltpu.VMEM((count, HEAD_WIDTH), jnp.bfloat16),
            pltpu.VMEM((count, 2 * HEAD_WIDTH), jnp.bfloat16),
        ],
        compiler_params=pltpu.CompilerParams(vmem_limit_bytes=ATTEND_LIMIT),
        cost_estimate=pl.CostEstimate(
            flops=4 * rows * block * count,
            bytes_accessed=8 * rows * block,
            transcendentals=rows * count * block // HEAD_WIDTH,
        ),
        name="attend",
    )(*operands)


def per_device(hidden, queries, layout, boundary, key_matrix, value_matrix):
    tokens, order, start_doc = hidden[0], layout[0], boundary[0]
    rows_here = tokens.shape[0]
    half = rows_here // 2
    kv_width = key_matrix.shape[1]
    kv_heads = kv_width // HEAD_WIDTH
    ctx_count, dp_count = lax.axis_size("ctx"), lax.axis_size("dp")
    here, window = lax.axis_index("ctx"), lax.axis_index("dp")
    core = here % 2
    chips = ctx_count // 2
    masks = [1 << bit for bit in range(1, ctx_count.bit_length() - 1)]

    is_keys = core == 0
    mine = jnp.where(is_keys, key_matrix, value_matrix)
    theirs = swapped(jnp.where(is_keys, value_matrix, key_matrix), 1)
    matrix = jnp.concatenate((jnp.where(is_keys, mine, theirs), jnp.where(is_keys, theirs, mine)), axis=0)
    (other_tokens, _) = lax.optimization_barrier((tokens, theirs))
    other_tokens = swapped(other_tokens, 1)

    depth = matrix.shape[0] // 2
    far_masks = [1 << bit for bit in reversed(range(dp_count.bit_length() - 1))]

    def renamed(names, mask):
        return [(by, xor ^ mask, part) for by, xor, part in names]

    def all_names(names):
        for mask in masks[2:]:
            names = names + renamed(names, mask)
        low, high = masks[:2]
        return names + renamed(names, low) + renamed(names, high) + renamed(names, low ^ high)

    def nearby(rows):
        for mask in masks[2:]:
            rows = jnp.concatenate((rows, swapped(rows, mask)), axis=0)
        return [rows, swapped(rows, masks[0]), swapped(rows, masks[1])]

    def onward(pieces):
        rows, beside, above = pieces
        cut = rows.shape[0] // 2
        return [rows, beside, above, swapped(beside[:cut], masks[1]), swapped(above[cut:], masks[0])]

    def together(values, *others):
        joined = lax.optimization_barrier((*values, *others))
        return joined[: len(values)]

    plane = list(range(2, ctx_count, 2))

    def sent_round(made):
        return [made] + [swapped(made, xor) for xor in plane]

    def both_sides(parts):
        held = jnp.concatenate(parts, axis=0)
        return held, swapped(held, 1)

    sources = [(here // 2 * 2 ^ xor) + side for xor in [0] + plane for side in range(2)]
    block_ids = jnp.arange(order.shape[0], dtype=jnp.int32)

    def positions(devices):
        blocks = (jnp.stack(devices)[:, None] * 2 + jnp.arange(2)[None, :]).reshape(-1)
        looked = jnp.sum(jnp.where(blocks[:, None] == block_ids[None, :], order[None, :], 0), axis=1)
        return (looked[:, None] * half + jnp.arange(half, dtype=jnp.int32)[None, :]).reshape(-1)

    query_pos = positions([here])[:, None]
    key_pos = positions(sources)[None, :]
    allowed = (key_pos <= query_pos) & ((key_pos >= start_doc) | (query_pos < start_doc))
    bias = jnp.where(allowed, 0.0, -jnp.inf).astype(jnp.float32)

    cuts = [(0, 1), (1, kv_heads - 2), (kv_heads - 1, 1)]

    def wide(value, first, count):
        return value[:, first * HEAD_WIDTH : (first + count) * HEAD_WIDTH]

    names = all_names([(0, 0, part) for part in range(2)])
    column = [0]
    for mask in far_masks:
        column = column + [by ^ mask for by in column]
    names += all_names([(by, 0, part) for by in column[1:] for part in range(2)])
    starts = jnp.stack(
        [core] + [((window ^ by) * chips + ((here ^ xor) // 2)) * 2 + part for by, xor, part in names]
    ).astype(jnp.int32)
    ordered = depth % 128 == 0
    if ordered:
        arranged = arrange(starts, tokens, other_tokens)
    else:
        both = jnp.where(is_keys, 0, 1)
        arranged = jnp.stack((tokens, other_tokens))[jnp.stack((both, 1 - both))].reshape(2 * rows_here, -1)
        order_of = jnp.argsort(starts[1:])

    def project_cut(index, pieces):
        first, count = cuts[index]
        if ordered:
            return project(arranged, own_depth, pieces, own_total, first * HEAD_WIDTH, jnp.bfloat16)
        blocks = jnp.concatenate([wide(rows, first, count) for rows in own] + list(pieces), axis=0)
        blocks = jnp.take(blocks.reshape(-1, depth, count * HEAD_WIDTH), order_of, axis=0)
        return project(arranged, 0, [blocks.reshape(-1, count * HEAD_WIDTH)], None, 0, jnp.bfloat16)

    def attend_head(index, head, held, result):
        return attend(core[None], bias, queries[0], held, result, cuts[index][0], head, kv_heads)

    def columns_of(index):
        return wide(matrix, *cuts[index])

    def along(held, mask):
        return held + [across(held[0] if len(held) == 1 else jnp.concatenate(held, axis=0), mask)]

    def rest(held):
        return jnp.concatenate(held[1:], axis=0)

    own = nearby(matrix)
    column_a = along([columns_of(0)], far_masks[0])
    (start_b, *column_a) = together([columns_of(1), *column_a])
    for mask in far_masks[1:-1]:
        column_a = along(column_a, mask)
    column_a = along(column_a, far_masks[-1])
    column_b = along([start_b], far_masks[0])
    own = onward(own)
    own_depth = sum(rows.shape[0] for rows in own)
    (arranged, *column_a) = together([arranged, *column_a])
    near_a = nearby(rest(column_a))

    tick = list(together([*near_a, *own, *column_b, columns_of(2)]))
    near_a, own, column_b, column_c = tick[:3], tick[3:8], tick[8:-1], tick[-1:]
    all_a = onward(near_a)
    for mask in far_masks[1:]:
        column_b = along(column_b, mask)
    for mask in far_masks:
        column_c = along(column_c, mask)
    own_total = project(arranged, 0, own, None, 0, jnp.float32) if ordered else matrix

    tick = list(together([*all_a, own_total]))
    all_a, own_total = tick[:5], tick[5]
    parts_a = sent_round(project_cut(0, all_a))
    tick = list(together([*column_b, parts_a[0]]))
    column_b, parts_a[0] = tick[:-1], tick[-1]
    near_b = nearby(rest(column_b))
    result = attend_head(0, 0, both_sides(parts_a), None)

    tick = list(together([*near_b, *column_c, result]))
    near_b, column_c, result = tick[:3], tick[3:-1], tick[-1]
    all_b = onward(near_b)
    near_c = nearby(rest(column_c))

    tick = list(together([*all_b, *near_c]))
    all_b, near_c = tick[:5], tick[5:8]
    all_c = onward(near_c)
    parts_b = sent_round(project_cut(1, all_b))

    tick = list(together([*all_c, parts_b[0]]))
    all_c, parts_b[0] = tick[:5], tick[5]
    parts_c = sent_round(project_cut(2, all_c))
    side_b = both_sides(parts_b)
    side_b = together(side_b, parts_c[0])
    for head in range(cuts[1][1]):
        if head == cuts[1][1] - 1:
            (result, *parts_c) = together([result, *parts_c])
            side_c = both_sides(parts_c)
        result = attend_head(1, head, side_b, result)
    result = attend_head(2, 0, side_c, result)
    return result[None]


def solution(mesh):
    in_specs = (
        P("dp", "ctx", None),
        P("dp", "ctx", None),
        P("dp", None),
        P("dp"),
        P(("dp", "ctx"), None),
        P(("dp", "ctx"), None),
    )
    out_specs = P("dp", "ctx", None)
    return jax.shard_map(
        per_device, mesh=mesh, in_specs=in_specs, out_specs=out_specs, check_vma=False
    )
```

profile of v0, /device:TPU:0, one launch (start us, length us, event | category | flops | bytes accessed | tf_op | source)
XLA Modules:
  0.0 137.6 jit_solution(9485406596878924119)
XLA Ops:
  5.2 3.8 %collective-permute-start.2 = (bf16[512,128]{1,0:T(8,128)(2,1)S(1)}, bf16[512,128]{1,0:T(8,128)(2,1)S(1)}, u32[]{:S(2)}, u32[]{:S(2)}) collective-permute-start(bf16[512,128]{1,0:T(8,128)(2,1)S(1)} %get-tuple-element.60), channel_id=1, source_target_pairs={{0,16},{8,24},{16,0},{24,8},{1,17},{9,25},{17,1},{25,9},{2,18},{10... | collective-permute-start | bytes 393224 | tf_op jit(solution)/shard_map/ppermute | solution.py:24
  9.0 1.6 %collective-permute-start.6 = (bf16[512,512]{1,0:T(8,128)(2,1)S(1)}, bf16[512,512]{1,0:T(8,128)(2,1)S(1)}, u32[]{:S(2)}, u32[]{:S(2)}) collective-permute-start(bf16[512,512]{1,0:T(8,128)(2,1)S(1)} %pad_maximum_fusion.refs_0_), channel_id=1, source_target_pairs={{0,2},{1,3},{2,0},{3,1},{4,6},{5,7},{6,4},{7,5},{8,10},{9,11},{10,... | collective-permute-start | bytes 1572872 | tf_op jit(solution)/shard_map/ppermute | solution.py:19
  12.1 3.7 %collective-permute-done.2 = bf16[512,128]{1,0:T(8,128)(2,1)S(1)} collective-permute-done((bf16[512,128]{1,0:T(8,128)(2,1)S(1)}, bf16[512,128]{1,0:T(8,128)(2,1)S(1)}, u32[]{:S(2)}, u32[]{:S(2)}) %collective-permute-start.2) | collective-permute-done | bytes 131104 | tf_op jit(solution)/shard_map/ppermute | solution.py:24
  17.8 3.4 %collective-permute-start.10 = (bf16[512,256]{1,0:T(8,128)(2,1)S(1)}, bf16[512,256]{1,0:T(8,128)(2,1)S(1)}, u32[]{:S(2)}, u32[]{:S(2)}) collective-permute-start(bf16[512,256]{1,0:T(8,128)(2,1)S(1)} %fusion), channel_id=1, source_target_pairs={{0,16},{8,24},{16,0},{24,8},{1,17},{9,25},{17,1},{25,9},{2,18},{10... | collective-permute-start | bytes 786440 | tf_op jit(solution)/shard_map/ppermute | solution.py:24
  21.1 1.9 %collective-permute-done.6.refs_1_ = bf16[512,512]{1,0:T(8,128)(2,1)S(1)} collective-permute-done((bf16[512,512]{1,0:T(8,128)(2,1)S(1)}, bf16[512,512]{1,0:T(8,128)(2,1)S(1)}, u32[]{:S(2)}, u32[]{:S(2)}) %collective-permute-start.6) | collective-permute-done | bytes 524320 | tf_op jit(solution)/shard_map/ppermute | solution.py:19
  23.0 1.6 %collective-permute-start.8 = (bf16[256,512]{1,0:T(8,128)(2,1)S(1)}, bf16[256,512]{1,0:T(8,128)(2,1)S(1)}, u32[]{:S(2)}, u32[]{:S(2)}) collective-permute-start(bf16[256,512]{1,0:T(8,128)(2,1)S(1)} %slice.48), channel_id=1, source_target_pairs={{0,4},{1,5},{2,6},{3,7},{4,0},{5,1},{6,2},{7,3},{8,12},{9,13},{10,... | collective-permute-start | bytes 786440 | tf_op jit(solution)/shard_map/ppermute | solution.py:19
  24.6 1.6 %collective-permute-start.9 = (bf16[256,512]{1,0:T(8,128)(2,1)S(1)}, bf16[256,512]{1,0:T(8,128)(2,1)S(1)}, u32[]{:S(2)}, u32[]{:S(2)}) collective-permute-start(bf16[256,512]{1,0:T(8,128)(2,1)S(1)} %slice.49), channel_id=1, source_target_pairs={{0,2},{1,3},{2,0},{3,1},{4,6},{5,7},{6,4},{7,5},{8,10},{9,11},{10,... | collective-permute-start | bytes 786440 | tf_op jit(solution)/shard_map/ppermute | solution.py:19
  26.2 2.2 %copy-done.1 = bf16[1,256,8192]{2,1,0:T(8,128)(2,1)S(1)} copy-done((bf16[1,256,8192]{2,1,0:T(8,128)(2,1)S(1)}, bf16[1,256,8192]{2,1,0:T(8,128)(2,1)}, u32[]{:S(2)}) %copy-start.1) | copy-done | bytes 4194328
  28.4 4.2 %arrange.1.tokens = bf16[512,8192]{1,0:T(8,128)(2,1)S(1)} custom-call(s32[33]{0:T(128)S(1)} %stack.168.starts, bf16[256,8192]{1,0:T(8,128)(2,1)S(1)} %bitcast.61, bf16[256,8192]{1,0:T(8,128)(2,1)} %collective-permute-done.1.other_ref), custom_call_target="tpu_custom_call" | custom-call | bytes 16777216 | tf_op jit(solution)/shard_map/arrange/pallas_call | solution.py:52
  34.4 8.0 %collective-permute-done.4.refs_1_ = bf16[1536,128]{1,0:T(8,128)(2,1)S(1)} collective-permute-done((bf16[1536,128]{1,0:T(8,128)(2,1)S(1)}, bf16[1536,128]{1,0:T(8,128)(2,1)S(1)}, u32[]{:S(2)}, u32[]{:S(2)}) %collective-permute-start.4) | collective-permute-done | bytes 393248 | tf_op jit(solution)/shard_map/ppermute | solution.py:19
  42.7 1.6 %collective-permute-start.11 = (bf16[1024,256]{1,0:T(8,128)(2,1)S(1)}, bf16[1024,256]{1,0:T(8,128)(2,1)S(1)}, u32[]{:S(2)}, u32[]{:S(2)}) collective-permute-start(bf16[1024,256]{1,0:T(8,128)(2,1)S(1)} %pad_maximum_fusion.1), channel_id=1, source_target_pairs={{0,8},{8,0},{16,24},{24,16},{1,9},{9,1},{17,25},{25,17},{2,10},{10... | collective-permute-start | bytes 1572872 | tf_op jit(solution)/shard_map/ppermute | solution.py:24
  48.2 1.9 %collective-permute-done.12.refs_3_ = bf16[768,128]{1,0:T(8,128)(2,1)S(1)} collective-permute-done((bf16[768,128]{1,0:T(8,128)(2,1)S(1)}, bf16[768,128]{1,0:T(8,128)(2,1)S(1)}, u32[]{:S(2)}, u32[]{:S(2)}) %collective-permute-start.12) | collective-permute-done | bytes 196640 | tf_op jit(solution)/shard_map/ppermute | solution.py:19
  51.3 1.8 %project.5 = bf16[512,128]{1,0:T(8,128)(2,1)S(1)} custom-call(bf16[512,8192]{1,0:T(8,128)(2,1)S(1)} %arrange.1.tokens, bf16[1536,128]{1,0:T(8,128)(2,1)S(1)} %constant_dynamic-update-slice_fusion.refs_0_, bf16[1536,128]{1,0:T(8,128)(2,1)S(1)} %collective-permute-done.4.refs_1_, bf16[1536,128]{1,0:T(8,128)(2,1)S(1)} %collective-permute-done.5.refs_2_, ...), custom_call_target="tpu_custom_call" | custom-call | flops 805306368 | bytes 6291456 | tf_op jit(solution)/shard_map/project/pallas_call | solution.py:81
  54.1 1.6 %collective-permute-start.19 = (bf16[512,128]{1,0:T(8,128)(2,1)S(1)}, bf16[512,128]{1,0:T(8,128)(2,1)S(1)}, u32[]{:S(2)}, u32[]{:S(2)}) collective-permute-start(bf16[512,128]{1,0:T(8,128)(2,1)S(1)} %project.5), channel_id=1, source_target_pairs={{0,4},{1,5},{2,6},{3,7},{4,0},{5,1},{6,2},{7,3},{8,12},{9,13},{10,... | collective-permute-start | bytes 393224 | tf_op jit(solution)/shard_map/ppermute | solution.py:19
  57.1 1.5 %collective-permute-start.14 = (bf16[1536,256]{1,0:T(8,128)(2,1)S(1)}, bf16[1536,256]{1,0:T(8,128)(2,1)S(1)}, u32[]{:S(2)}, u32[]{:S(2)}) collective-permute-start(bf16[1536,256]{1,0:T(8,128)(2,1)S(1)} %constant_dynamic-update-slice_fusion.2.refs_0_), channel_id=1, source_target_pairs={{0,2},{1,3},{2,0},{3,1},{4,6},{5,7},{6,4},{7,5},{8,10},{9,11},{10,... | collective-permute-start | bytes 2359304 | tf_op jit(solution)/shard_map/ppermute | solution.py:19
  60.6 2.4 %collective-permute-done.20 = bf16[512,128]{1,0:T(8,128)(2,1)S(1)} collective-permute-done((bf16[512,128]{1,0:T(8,128)(2,1)S(1)}, bf16[512,128]{1,0:T(8,128)(2,1)S(1)}, u32[]{:S(2)}, u32[]{:S(2)}) %collective-permute-start.20) | collective-permute-done | bytes 131104 | tf_op jit(solution)/shard_map/ppermute | solution.py:19
  65.0 7.0 %attend.4.refs_0_ = bf16[256,4096]{1,0:T(8,128)(2,1)} custom-call(s32[1]{0:T(128)} %bitcast.core, f32[256,2048]{1,0:T(8,128)S(1)} %and_select_fusion.bias, bf16[256,4096]{1,0:T(8,128)(2,1)S(1)} %bitcast.56, bf16[2048,128]{1,0:T(8,128)(2,1)S(1)} %constant_dynamic-update-slice_fusion.4.held, bf16[2048,128]{1,0:T(8,128)(2,1)S(1)} %collective-permute-done.21.sent), custom_call_target="tpu_custom_call" | custom-call | flops 2147483648 | bytes 2097152 | tf_op jit(solution)/shard_map/attend/pallas_call | solution.py:129
  72.0 3.5 %collective-permute-done.14.refs_1_ = bf16[1536,256]{1,0:T(8,128)(2,1)S(1)} collective-permute-done((bf16[1536,256]{1,0:T(8,128)(2,1)S(1)}, bf16[1536,256]{1,0:T(8,128)(2,1)S(1)}, u32[]{:S(2)}, u32[]{:S(2)}) %collective-permute-start.14) | collective-permute-done | bytes 786464 | tf_op jit(solution)/shard_map/ppermute | solution.py:19
  79.6 1.7 %collective-permute-start.23 = (bf16[768,256]{1,0:T(8,128)(2,1)S(1)}, bf16[768,256]{1,0:T(8,128)(2,1)S(1)}, u32[]{:S(2)}, u32[]{:S(2)}) collective-permute-start(bf16[768,256]{1,0:T(8,128)(2,1)S(1)} %slice.41), channel_id=1, source_target_pairs={{0,2},{1,3},{2,0},{3,1},{4,6},{5,7},{6,4},{7,5},{8,10},{9,11},{10,... | collective-permute-start | bytes 1179656 | tf_op jit(solution)/shard_map/ppermute | solution.py:19
  81.3 7.8 %collective-permute-done.24.refs_1_ = bf16[1536,128]{1,0:T(8,128)(2,1)S(1)} collective-permute-done((bf16[1536,128]{1,0:T(8,128)(2,1)S(1)}, bf16[1536,128]{1,0:T(8,128)(2,1)S(1)}, u32[]{:S(2)}, u32[]{:S(2)}) %collective-permute-start.24) | collective-permute-done | bytes 393248 | tf_op jit(solution)/shard_map/ppermute | solution.py:19
  89.5 5.6 %collective-permute-done.22.refs_3_ = bf16[768,256]{1,0:T(8,128)(2,1)S(1)} collective-permute-done((bf16[768,256]{1,0:T(8,128)(2,1)S(1)}, bf16[768,256]{1,0:T(8,128)(2,1)S(1)}, u32[]{:S(2)}, u32[]{:S(2)}) %collective-permute-start.22) | collective-permute-done | bytes 393248 | tf_op jit(solution)/shard_map/ppermute | solution.py:19
  95.5 1.7 %collective-permute-start.27 = (bf16[768,128]{1,0:T(8,128)(2,1)S(1)}, bf16[768,128]{1,0:T(8,128)(2,1)S(1)}, u32[]{:S(2)}, u32[]{:S(2)}) collective-permute-start(bf16[768,128]{1,0:T(8,128)(2,1)S(1)} %slice.43), channel_id=1, source_target_pairs={{0,2},{1,3},{2,0},{3,1},{4,6},{5,7},{6,4},{7,5},{8,10},{9,11},{10,... | collective-permute-start | bytes 589832 | tf_op jit(solution)/shard_map/ppermute | solution.py:19
  97.2 2.0 %project.6 = bf16[512,256]{1,0:T(8,128)(2,1)S(1)} custom-call(bf16[512,8192]{1,0:T(8,128)(2,1)S(1)} %arrange.1.tokens, bf16[1536,256]{1,0:T(8,128)(2,1)S(1)} %constant_dynamic-update-slice_fusion.2.refs_0_, bf16[1536,256]{1,0:T(8,128)(2,1)S(1)} %collective-permute-done.14.refs_1_, bf16[1536,256]{1,0:T(8,128)(2,1)S(1)} %collective-permute-done.15.refs_2_, ...), custom_call_target="tpu_custom_call" | custom-call | flops 1610612736 | bytes 6291456 | tf_op jit(solution)/shard_map/project/pallas_call | solution.py:81
  99.6 1.7 %collective-permute-start.29 = (bf16[512,256]{1,0:T(8,128)(2,1)S(1)}, bf16[512,256]{1,0:T(8,128)(2,1)S(1)}, u32[]{:S(2)}, u32[]{:S(2)}) collective-permute-start(bf16[512,256]{1,0:T(8,128)(2,1)S(1)} %project.6), channel_id=1, source_target_pairs={{0,4},{1,5},{2,6},{3,7},{4,0},{5,1},{6,2},{7,3},{8,12},{9,13},{10,... | collective-permute-start | bytes 786440 | tf_op jit(solution)/shard_map/ppermute | solution.py:19
  103.4 2.9 %collective-permute-done.28 = bf16[512,256]{1,0:T(8,128)(2,1)S(1)} collective-permute-done((bf16[512,256]{1,0:T(8,128)(2,1)S(1)}, bf16[512,256]{1,0:T(8,128)(2,1)S(1)}, u32[]{:S(2)}, u32[]{:S(2)}) %collective-permute-start.28) | collective-permute-done | bytes 262176 | tf_op jit(solution)/shard_map/ppermute | solution.py:19
  106.4 2.4 %collective-permute-done.29 = bf16[512,256]{1,0:T(8,128)(2,1)S(1)} collective-permute-done((bf16[512,256]{1,0:T(8,128)(2,1)S(1)}, bf16[512,256]{1,0:T(8,128)(2,1)S(1)}, u32[]{:S(2)}, u32[]{:S(2)}) %collective-permute-start.29) | collective-permute-done | bytes 262176 | tf_op jit(solution)/shard_map/ppermute | solution.py:19
  108.8 1.5 %collective-permute-done.30 = bf16[512,256]{1,0:T(8,128)(2,1)S(1)} collective-permute-done((bf16[512,256]{1,0:T(8,128)(2,1)S(1)}, bf16[512,256]{1,0:T(8,128)(2,1)S(1)}, u32[]{:S(2)}, u32[]{:S(2)}) %collective-permute-start.30) | collective-permute-done | bytes 262176 | tf_op jit(solution)/shard_map/ppermute | solution.py:19
  110.4 1.8 %project.7 = bf16[512,128]{1,0:T(8,128)(2,1)S(1)} custom-call(bf16[512,8192]{1,0:T(8,128)(2,1)S(1)} %arrange.1.tokens, bf16[1536,128]{1,0:T(8,128)(2,1)S(1)} %constant_dynamic-update-slice_fusion.8.refs_0_, bf16[1536,128]{1,0:T(8,128)(2,1)S(1)} %collective-permute-done.24.refs_1_, bf16[1536,128]{1,0:T(8,128)(2,1)S(1)} %collective-permute-done.25.refs_2_, ...), custom_call_target="tpu_custom_call" | custom-call | flops 805306368 | bytes 6291456 | tf_op jit(solution)/shard_map/project/pallas_call | solution.py:81
  112.9 1.7 %collective-permute-start.33 = (bf16[512,128]{1,0:T(8,128)(2,1)S(1)}, bf16[512,128]{1,0:T(8,128)(2,1)S(1)}, u32[]{:S(2)}, u32[]{:S(2)}) collective-permute-start(bf16[512,128]{1,0:T(8,128)(2,1)S(1)} %project.7), channel_id=1, source_target_pairs={{0,4},{1,5},{2,6},{3,7},{4,0},{5,1},{6,2},{7,3},{8,12},{9,13},{10,... | collective-permute-start | bytes 393224 | tf_op jit(solution)/shard_map/ppermute | solution.py:19
  115.8 7.2 %attend.5.refs_0_ = bf16[256,4096]{1,0:T(8,128)(2,1)} custom-call(s32[1]{0:T(128)} %bitcast.core, f32[256,2048]{1,0:T(8,128)S(1)} %and_select_fusion.bias, bf16[256,4096]{1,0:T(8,128)(2,1)S(1)} %bitcast.57, bf16[2048,256]{1,0:T(8,128)(2,1)S(1)} %constant_dynamic-update-slice_fusion.10.held, ...), custom_call_target="tpu_custom_call", output_to_operand_aliasing={{}: (5, {})} | custom-call | flops 2147483648 | bytes 2097152 | tf_op jit(solution)/shard_map/attend/pallas_call | solution.py:129
  123.1 7.4 %attend.6.refs_0_ = bf16[256,4096]{1,0:T(8,128)(2,1)} custom-call(s32[1]{0:T(128)} %bitcast.core, f32[256,2048]{1,0:T(8,128)S(1)} %and_select_fusion.bias, bf16[256,4096]{1,0:T(8,128)(2,1)S(1)} %bitcast.58, bf16[2048,256]{1,0:T(8,128)(2,1)S(1)} %constant_dynamic-update-slice_fusion.10.held, ...), custom_call_target="tpu_custom_call", output_to_operand_aliasing={{}: (5, {})} | custom-call | flops 2147483648 | bytes 2097152 | tf_op jit(solution)/shard_map/attend/pallas_call | solution.py:129
  130.6 7.0 %attend.7 = bf16[256,4096]{1,0:T(8,128)(2,1)} custom-call(s32[1]{0:T(128)} %bitcast.core, f32[256,2048]{1,0:T(8,128)S(1)} %and_select_fusion.bias, bf16[256,4096]{1,0:T(8,128)(2,1)S(1)} %bitcast.59, bf16[2048,128]{1,0:T(8,128)(2,1)S(1)} %constant_dynamic-update-slice_fusion.14.held, ...), custom_call_target="tpu_custom_call", output_to_operand_aliasing={{}: (5, {})} | custom-call | flops 2147483648 | bytes 2097152 | tf_op jit(solution)/shard_map/attend/pallas_call | solution.py:129
  (104 shorter events, 30.7 us)
Async XLA Ops:
  2.7 23.5 %collective-permute-start.1 = (bf16[256,8192]{1,0:T(8,128)(2,1)}, bf16[256,8192]{1,0:T(8,128)(2,1)}, u32[]{:S(2)}, u32[]{:S(2)}) collective-permute-start(bf16[256,8192]{1,0:T(8,128)(2,1)} %bitcast.60), channel_id=1, source_target_pairs={{0,1},{1,0},{2,3},{3,2},{4,5},{5,4},{6,7},{7,6},{8,9},{9,8},{10,11... | collective-permute-start | bytes 12582920 | tf_op jit(solution)/shard_map/ppermute | solution.py:19
  5.2 10.6 %collective-permute-start.2 = (bf16[512,128]{1,0:T(8,128)(2,1)S(1)}, bf16[512,128]{1,0:T(8,128)(2,1)S(1)}, u32[]{:S(2)}, u32[]{:S(2)}) collective-permute-start(bf16[512,128]{1,0:T(8,128)(2,1)S(1)} %get-tuple-element.60), channel_id=1, source_target_pairs={{0,16},{8,24},{16,0},{24,8},{1,17},{9,25},{17,1},{25,9},{2,18},{10... | collective-permute-start | bytes 393224 | tf_op jit(solution)/shard_map/ppermute | solution.py:24
  9.0 14.0 %collective-permute-start.6 = (bf16[512,512]{1,0:T(8,128)(2,1)S(1)}, bf16[512,512]{1,0:T(8,128)(2,1)S(1)}, u32[]{:S(2)}, u32[]{:S(2)}) collective-permute-start(bf16[512,512]{1,0:T(8,128)(2,1)S(1)} %pad_maximum_fusion.refs_0_), channel_id=1, source_target_pairs={{0,2},{1,3},{2,0},{3,1},{4,6},{5,7},{6,4},{7,5},{8,10},{9,11},{10,... | collective-permute-start | bytes 1572872 | tf_op jit(solution)/shard_map/ppermute | solution.py:19
  10.6 14.0 %collective-permute-start.7 = (bf16[512,512]{1,0:T(8,128)(2,1)S(1)}, bf16[512,512]{1,0:T(8,128)(2,1)S(1)}, u32[]{:S(2)}, u32[]{:S(2)}) collective-permute-start(bf16[512,512]{1,0:T(8,128)(2,1)S(1)} %pad_maximum_fusion.refs_0_), channel_id=1, source_target_pairs={{0,4},{1,5},{2,6},{3,7},{4,0},{5,1},{6,2},{7,3},{8,12},{9,13},{10,... | collective-permute-start | bytes 1572872 | tf_op jit(solution)/shard_map/ppermute | solution.py:19
  15.8 16.8 %collective-permute-start.3 = (bf16[1024,128]{1,0:T(8,128)(2,1)S(1)}, bf16[1024,128]{1,0:T(8,128)(2,1)S(1)}, u32[]{:S(2)}, u32[]{:S(2)}) collective-permute-start(bf16[1024,128]{1,0:T(8,128)(2,1)S(1)} %pad_maximum_fusion.2), channel_id=1, source_target_pairs={{0,8},{8,0},{16,24},{24,16},{1,9},{9,1},{17,25},{25,17},{2,10},{10... | collective-permute-start | bytes 786440 | tf_op jit(solution)/shard_map/ppermute | solution.py:24
  17.8 16.6 %collective-permute-start.10 = (bf16[512,256]{1,0:T(8,128)(2,1)S(1)}, bf16[512,256]{1,0:T(8,128)(2,1)S(1)}, u32[]{:S(2)}, u32[]{:S(2)}) collective-permute-start(bf16[512,256]{1,0:T(8,128)(2,1)S(1)} %fusion), channel_id=1, source_target_pairs={{0,16},{8,24},{16,0},{24,8},{1,17},{9,25},{17,1},{25,9},{2,18},{10... | collective-permute-start | bytes 786440 | tf_op jit(solution)/shard_map/ppermute | solution.py:24
  23.0 11.4 %collective-permute-start.8 = (bf16[256,512]{1,0:T(8,128)(2,1)S(1)}, bf16[256,512]{1,0:T(8,128)(2,1)S(1)}, u32[]{:S(2)}, u32[]{:S(2)}) collective-permute-start(bf16[256,512]{1,0:T(8,128)(2,1)S(1)} %slice.48), channel_id=1, source_target_pairs={{0,4},{1,5},{2,6},{3,7},{4,0},{5,1},{6,2},{7,3},{8,12},{9,13},{10,... | collective-permute-start | bytes 786440 | tf_op jit(solution)/shard_map/ppermute | solution.py:19
  24.6 9.8 %collective-permute-start.9 = (bf16[256,512]{1,0:T(8,128)(2,1)S(1)}, bf16[256,512]{1,0:T(8,128)(2,1)S(1)}, u32[]{:S(2)}, u32[]{:S(2)}) collective-permute-start(bf16[256,512]{1,0:T(8,128)(2,1)S(1)} %slice.49), channel_id=1, source_target_pairs={{0,2},{1,3},{2,0},{3,1},{4,6},{5,7},{6,4},{7,5},{8,10},{9,11},{10,... | collective-permute-start | bytes 786440 | tf_op jit(solution)/shard_map/ppermute | solution.py:19
  32.7 9.8 %collective-permute-start.4 = (bf16[1536,128]{1,0:T(8,128)(2,1)S(1)}, bf16[1536,128]{1,0:T(8,128)(2,1)S(1)}, u32[]{:S(2)}, u32[]{:S(2)}) collective-permute-start(bf16[1536,128]{1,0:T(8,128)(2,1)S(1)} %constant_dynamic-update-slice_fusion.refs_0_), channel_id=1, source_target_pairs={{0,2},{1,3},{2,0},{3,1},{4,6},{5,7},{6,4},{7,5},{8,10},{9,11},{10,... | collective-permute-start | bytes 1179656 | tf_op jit(solution)/shard_map/ppermute | solution.py:19
  33.2 9.4 %collective-permute-start.5 = (bf16[1536,128]{1,0:T(8,128)(2,1)S(1)}, bf16[1536,128]{1,0:T(8,128)(2,1)S(1)}, u32[]{:S(2)}, u32[]{:S(2)}) collective-permute-start(bf16[1536,128]{1,0:T(8,128)(2,1)S(1)} %constant_dynamic-update-slice_fusion.refs_0_), channel_id=1, source_target_pairs={{0,4},{1,5},{2,6},{3,7},{4,0},{5,1},{6,2},{7,3},{8,12},{9,13},{10,... | collective-permute-start | bytes 1179656 | tf_op jit(solution)/shard_map/ppermute | solution.py:19
  42.7 14.3 %collective-permute-start.11 = (bf16[1024,256]{1,0:T(8,128)(2,1)S(1)}, bf16[1024,256]{1,0:T(8,128)(2,1)S(1)}, u32[]{:S(2)}, u32[]{:S(2)}) collective-permute-start(bf16[1024,256]{1,0:T(8,128)(2,1)S(1)} %pad_maximum_fusion.1), channel_id=1, source_target_pairs={{0,8},{8,0},{16,24},{24,16},{1,9},{9,1},{17,25},{25,17},{2,10},{10... | collective-permute-start | bytes 1572872 | tf_op jit(solution)/shard_map/ppermute | solution.py:24
  45.6 5.7 %collective-permute-start.13 = (bf16[768,128]{1,0:T(8,128)(2,1)S(1)}, bf16[768,128]{1,0:T(8,128)(2,1)S(1)}, u32[]{:S(2)}, u32[]{:S(2)}) collective-permute-start(bf16[768,128]{1,0:T(8,128)(2,1)S(1)} %slice.39), channel_id=1, source_target_pairs={{0,2},{1,3},{2,0},{3,1},{4,6},{5,7},{6,4},{7,5},{8,10},{9,11},{10,... | collective-permute-start | bytes 589832 | tf_op jit(solution)/shard_map/ppermute | solution.py:19
  46.7 16.4 %collective-permute-start.16 = (bf16[512,128]{1,0:T(8,128)(2,1)S(1)}, bf16[512,128]{1,0:T(8,128)(2,1)S(1)}, u32[]{:S(2)}, u32[]{:S(2)}) collective-permute-start(bf16[512,128]{1,0:T(8,128)(2,1)S(1)} %get-tuple-element.84), channel_id=1, source_target_pairs={{0,16},{8,24},{16,0},{24,8},{1,17},{9,25},{17,1},{25,9},{2,18},{10... | collective-permute-start | bytes 393224 | tf_op jit(solution)/shard_map/ppermute | solution.py:24
  53.1 6.4 %collective-permute-start.18 = (bf16[512,128]{1,0:T(8,128)(2,1)S(1)}, bf16[512,128]{1,0:T(8,128)(2,1)S(1)}, u32[]{:S(2)}, u32[]{:S(2)}) collective-permute-start(bf16[512,128]{1,0:T(8,128)(2,1)S(1)} %project.5), channel_id=1, source_target_pairs={{0,2},{1,3},{2,0},{3,1},{4,6},{5,7},{6,4},{7,5},{8,10},{9,11},{10,... | collective-permute-start | bytes 393224 | tf_op jit(solution)/shard_map/ppermute | solution.py:19
  54.1 6.5 %collective-permute-start.19 = (bf16[512,128]{1,0:T(8,128)(2,1)S(1)}, bf16[512,128]{1,0:T(8,128)(2,1)S(1)}, u32[]{:S(2)}, u32[]{:S(2)}) collective-permute-start(bf16[512,128]{1,0:T(8,128)(2,1)S(1)} %project.5), channel_id=1, source_target_pairs={{0,4},{1,5},{2,6},{3,7},{4,0},{5,1},{6,2},{7,3},{8,12},{9,13},{10,... | collective-permute-start | bytes 393224 | tf_op jit(solution)/shard_map/ppermute | solution.py:19
  55.7 7.3 %collective-permute-start.20 = (bf16[512,128]{1,0:T(8,128)(2,1)S(1)}, bf16[512,128]{1,0:T(8,128)(2,1)S(1)}, u32[]{:S(2)}, u32[]{:S(2)}) collective-permute-start(bf16[512,128]{1,0:T(8,128)(2,1)S(1)} %project.5), channel_id=1, source_target_pairs={{0,6},{1,7},{2,4},{3,5},{4,2},{5,3},{6,0},{7,1},{8,14},{9,15},{10,... | collective-permute-start | bytes 393224 | tf_op jit(solution)/shard_map/ppermute | solution.py:19
  57.1 18.5 %collective-permute-start.14 = (bf16[1536,256]{1,0:T(8,128)(2,1)S(1)}, bf16[1536,256]{1,0:T(8,128)(2,1)S(1)}, u32[]{:S(2)}, u32[]{:S(2)}) collective-permute-start(bf16[1536,256]{1,0:T(8,128)(2,1)S(1)} %constant_dynamic-update-slice_fusion.2.refs_0_), channel_id=1, source_target_pairs={{0,2},{1,3},{2,0},{3,1},{4,6},{5,7},{6,4},{7,5},{8,10},{9,11},{10,... | collective-permute-start | bytes 2359304 | tf_op jit(solution)/shard_map/ppermute | solution.py:19
  59.5 17.5 %collective-permute-start.15 = (bf16[1536,256]{1,0:T(8,128)(2,1)S(1)}, bf16[1536,256]{1,0:T(8,128)(2,1)S(1)}, u32[]{:S(2)}, u32[]{:S(2)}) collective-permute-start(bf16[1536,256]{1,0:T(8,128)(2,1)S(1)} %constant_dynamic-update-slice_fusion.2.refs_0_), channel_id=1, source_target_pairs={{0,4},{1,5},{2,6},{3,7},{4,0},{5,1},{6,2},{7,3},{8,12},{9,13},{10,... | collective-permute-start | bytes 2359304 | tf_op jit(solution)/shard_map/ppermute | solution.py:19
  63.1 8.9 %collective-permute-start.17 = (bf16[1024,128]{1,0:T(8,128)(2,1)S(1)}, bf16[1024,128]{1,0:T(8,128)(2,1)S(1)}, u32[]{:S(2)}, u32[]{:S(2)}) collective-permute-start(bf16[1024,128]{1,0:T(8,128)(2,1)S(1)} %pad_maximum_fusion.3), channel_id=1, source_target_pairs={{0,8},{8,0},{16,24},{24,16},{1,9},{9,1},{17,25},{25,17},{2,10},{10... | collective-permute-start | bytes 786440 | tf_op jit(solution)/shard_map/ppermute | solution.py:24
  77.0 12.1 %collective-permute-start.24 = (bf16[1536,128]{1,0:T(8,128)(2,1)S(1)}, bf16[1536,128]{1,0:T(8,128)(2,1)S(1)}, u32[]{:S(2)}, u32[]{:S(2)}) collective-permute-start(bf16[1536,128]{1,0:T(8,128)(2,1)S(1)} %constant_dynamic-update-slice_fusion.8.refs_0_), channel_id=1, source_target_pairs={{0,2},{1,3},{2,0},{3,1},{4,6},{5,7},{6,4},{7,5},{8,10},{9,11},{10,... | collective-permute-start | bytes 1179656 | tf_op jit(solution)/shard_map/ppermute | solution.py:19
  77.4 12.1 %collective-permute-start.25 = (bf16[1536,128]{1,0:T(8,128)(2,1)S(1)}, bf16[1536,128]{1,0:T(8,128)(2,1)S(1)}, u32[]{:S(2)}, u32[]{:S(2)}) collective-permute-start(bf16[1536,128]{1,0:T(8,128)(2,1)S(1)} %constant_dynamic-update-slice_fusion.8.refs_0_), channel_id=1, source_target_pairs={{0,4},{1,5},{2,6},{3,7},{4,0},{5,1},{6,2},{7,3},{8,12},{9,13},{10,... | collective-permute-start | bytes 1179656 | tf_op jit(solution)/shard_map/ppermute | solution.py:19
  78.3 16.8 %collective-permute-start.22 = (bf16[768,256]{1,0:T(8,128)(2,1)S(1)}, bf16[768,256]{1,0:T(8,128)(2,1)S(1)}, u32[]{:S(2)}, u32[]{:S(2)}) collective-permute-start(bf16[768,256]{1,0:T(8,128)(2,1)S(1)} %slice.40), channel_id=1, source_target_pairs={{0,4},{1,5},{2,6},{3,7},{4,0},{5,1},{6,2},{7,3},{8,12},{9,13},{10,... | collective-permute-start | bytes 1179656 | tf_op jit(solution)/shard_map/ppermute | solution.py:19
  79.6 15.5 %collective-permute-start.23 = (bf16[768,256]{1,0:T(8,128)(2,1)S(1)}, bf16[768,256]{1,0:T(8,128)(2,1)S(1)}, u32[]{:S(2)}, u32[]{:S(2)}) collective-permute-start(bf16[768,256]{1,0:T(8,128)(2,1)S(1)} %slice.41), channel_id=1, source_target_pairs={{0,2},{1,3},{2,0},{3,1},{4,6},{5,7},{6,4},{7,5},{8,10},{9,11},{10,... | collective-permute-start | bytes 1179656 | tf_op jit(solution)/shard_map/ppermute | solution.py:19
  95.1 8.0 %collective-permute-start.26 = (bf16[768,128]{1,0:T(8,128)(2,1)S(1)}, bf16[768,128]{1,0:T(8,128)(2,1)S(1)}, u32[]{:S(2)}, u32[]{:S(2)}) collective-permute-start(bf16[768,128]{1,0:T(8,128)(2,1)S(1)} %slice.42), channel_id=1, source_target_pairs={{0,4},{1,5},{2,6},{3,7},{4,0},{5,1},{6,2},{7,3},{8,12},{9,13},{10,... | collective-permute-start | bytes 589832 | tf_op jit(solution)/shard_map/ppermute | solution.py:19
  95.5 7.9 %collective-permute-start.27 = (bf16[768,128]{1,0:T(8,128)(2,1)S(1)}, bf16[768,128]{1,0:T(8,128)(2,1)S(1)}, u32[]{:S(2)}, u32[]{:S(2)}) collective-permute-start(bf16[768,128]{1,0:T(8,128)(2,1)S(1)} %slice.43), channel_id=1, source_target_pairs={{0,2},{1,3},{2,0},{3,1},{4,6},{5,7},{6,4},{7,5},{8,10},{9,11},{10,... | collective-permute-start | bytes 589832 | tf_op jit(solution)/shard_map/ppermute | solution.py:19
  99.2 7.2 %collective-permute-start.28 = (bf16[512,256]{1,0:T(8,128)(2,1)S(1)}, bf16[512,256]{1,0:T(8,128)(2,1)S(1)}, u32[]{:S(2)}, u32[]{:S(2)}) collective-permute-start(bf16[512,256]{1,0:T(8,128)(2,1)S(1)} %project.6), channel_id=1, source_target_pairs={{0,2},{1,3},{2,0},{3,1},{4,6},{5,7},{6,4},{7,5},{8,10},{9,11},{10,... | collective-permute-start | bytes 786440 | tf_op jit(solution)/shard_map/ppermute | solution.py:19
  99.6 9.1 %collective-permute-start.29 = (bf16[512,256]{1,0:T(8,128)(2,1)S(1)}, bf16[512,256]{1,0:T(8,128)(2,1)S(1)}, u32[]{:S(2)}, u32[]{:S(2)}) collective-permute-start(bf16[512,256]{1,0:T(8,128)(2,1)S(1)} %project.6), channel_id=1, source_target_pairs={{0,4},{1,5},{2,6},{3,7},{4,0},{5,1},{6,2},{7,3},{8,12},{9,13},{10,... | collective-permute-start | bytes 786440 | tf_op jit(solution)/shard_map/ppermute | solution.py:19
  101.3 9.0 %collective-permute-start.30 = (bf16[512,256]{1,0:T(8,128)(2,1)S(1)}, bf16[512,256]{1,0:T(8,128)(2,1)S(1)}, u32[]{:S(2)}, u32[]{:S(2)}) collective-permute-start(bf16[512,256]{1,0:T(8,128)(2,1)S(1)} %project.6), channel_id=1, source_target_pairs={{0,6},{1,7},{2,4},{3,5},{4,2},{5,3},{6,0},{7,1},{8,14},{9,15},{10,... | collective-permute-start | bytes 786440 | tf_op jit(solution)/shard_map/ppermute | solution.py:19
  112.2 10.7 %collective-permute-start.32 = (bf16[512,128]{1,0:T(8,128)(2,1)S(1)}, bf16[512,128]{1,0:T(8,128)(2,1)S(1)}, u32[]{:S(2)}, u32[]{:S(2)}) collective-permute-start(bf16[512,128]{1,0:T(8,128)(2,1)S(1)} %project.7), channel_id=1, source_target_pairs={{0,2},{1,3},{2,0},{3,1},{4,6},{5,7},{6,4},{7,5},{8,10},{9,11},{10,... | collective-permute-start | bytes 393224 | tf_op jit(solution)/shard_map/ppermute | solution.py:19
  112.9 10.1 %collective-permute-start.33 = (bf16[512,128]{1,0:T(8,128)(2,1)S(1)}, bf16[512,128]{1,0:T(8,128)(2,1)S(1)}, u32[]{:S(2)}, u32[]{:S(2)}) collective-permute-start(bf16[512,128]{1,0:T(8,128)(2,1)S(1)} %project.7), channel_id=1, source_target_pairs={{0,4},{1,5},{2,6},{3,7},{4,0},{5,1},{6,2},{7,3},{8,12},{9,13},{10,... | collective-permute-start | bytes 393224 | tf_op jit(solution)/shard_map/ppermute | solution.py:19
  114.6 8.3 %collective-permute-start.34 = (bf16[512,128]{1,0:T(8,128)(2,1)S(1)}, bf16[512,128]{1,0:T(8,128)(2,1)S(1)}, u32[]{:S(2)}, u32[]{:S(2)}) collective-permute-start(bf16[512,128]{1,0:T(8,128)(2,1)S(1)} %project.7), channel_id=1, source_target_pairs={{0,6},{1,7},{2,4},{3,5},{4,2},{5,3},{6,0},{7,1},{8,14},{9,15},{10,... | collective-permute-start | bytes 393224 | tf_op jit(solution)/shard_map/ppermute | solution.py:19
  123.0 7.5 %collective-permute-start.35 = (bf16[2048,128]{1,0:T(8,128)(2,1)S(1)}, bf16[2048,128]{1,0:T(8,128)(2,1)S(1)}, u32[]{:S(2)}, u32[]{:S(2)}) collective-permute-start(bf16[2048,128]{1,0:T(8,128)(2,1)S(1)} %constant_dynamic-update-slice_fusion.14.held), channel_id=1, source_target_pairs={{0,1},{1,0},{2,3},{3,2},{4,5},{5,4},{6,7},{7,6},{8,9},{9,8},{10,11... | collective-permute-start | bytes 1572872 | tf_op jit(solution)/shard_map/ppermute | solution.py:19
  (7 other events, 37.5 us)
where the time goes:
time: 138 us
  waiting for transfers between devices  48.7 us (35%)
  starting transfers between devices  41.1 us (30%)
  Pallas kernels  39.7 us (29%)
  other arithmetic  4.02 us (3%)
  local copies, waits for them, and re-layouts  2.97 us (2%)
    ppermute x30, waiting for transfers between devices, swapped(): return lax.ppermute(value, 'ctx', [(i, i ^ mask) for i in range(size)])  44.7 us
    ppermute x30, starting transfers between devices, swapped(): return lax.ppermute(value, 'ctx', [(i, i ^ mask) for i in range(size)])  30.7 us
    pallas_call x4, Pallas kernels, attend(): pl.pallas_call(functools.partial(attend_kernel, HEAD_WIDTH ** (-0.5) * LO...  28.7 us
    ppermute x6, starting transfers between devices, across(): return lax.ppermute(value, 'dp', [(i, i ^ mask) for i in range(size)])  10.5 us
    pallas_call x4, Pallas kernels, project(): pl.pallas_call(functools.partial(project_kernel, first, column, len(total...  6.8 us
    pallas_call x1, Pallas kernels, arrange(): pl.pallas_call(functools.partial(arrange_kernel, blocks), out_shape=jax.S...  4.21 us
    ppermute x6, waiting for transfers between devices, across(): return lax.ppermute(value, 'dp', [(i, i ^ mask) for i in range(size)])  4.02 us
  transfers between devices with their start and end apart: 36, of which 21 were waited for; matrix products, arithmetic and copies ran while one was open for 3% of the time, Pallas kernels for 24%

commit v1 on v0

v1 whole, which is shorter than its diff:
```python
import functools

import jax
import jax.numpy as jnp
from jax import lax
from jax.experimental import pallas as pl
from jax.experimental.pallas import tpu as pltpu
from jax.sharding import PartitionSpec as P

HEAD_WIDTH = 128
LOG2_E = 1.4426950408889634
ARRANGE_LIMIT = 12 * 2**20
PROJECT_LIMIT = 18 * 2**20
ATTEND_LIMIT = 14 * 2**20
REGROUP_LIMIT = 10 * 2**20


def swapped(value, mask):
    size = lax.axis_size("ctx")
    return lax.ppermute(value, "ctx", [(i, i ^ mask) for i in range(size)])


def across(value, mask):
    size = lax.axis_size("dp")
    return lax.ppermute(value, "dp", [(i, i ^ mask) for i in range(size)])


def arrange_kernel(blocks, starts, own_ref, other_ref, out_ref, sems):
    core = starts[0]
    rows = own_ref.shape[0]
    depth = own_ref.shape[1] // blocks
    copies = []
    for source, place in ((own_ref, core), (other_ref, 1 - core)):
        for index in range(blocks):
            first = pl.multiple_of(starts[1 + index] * depth, depth)
            copies.append(
                pltpu.make_async_copy(
                    source.at[:, pl.ds(first, depth)],
                    out_ref.at[pl.ds(pl.multiple_of(place * rows, rows), rows), pl.ds(index * depth, depth)],
                    sems.at[len(copies)],
                )
            )
    for copy in copies:
        copy.start()
    for copy in copies:
        copy.wait()


def arrange(starts, own, other):
    blocks = starts.shape[0] - 1
    rows, columns = own.shape
    anywhere = pl.BlockSpec(memory_space=pl.ANY)
    return pl.pallas_call(
        functools.partial(arrange_kernel, blocks),
        out_shape=jax.ShapeDtypeStruct((2 * rows, columns), own.dtype),
        in_specs=[pl.BlockSpec(memory_space=pltpu.SMEM), anywhere, anywhere],
        out_specs=pl.BlockSpec(memory_space=pltpu.VMEM),
        scratch_shapes=[pltpu.SemaphoreType.DMA((2 * blocks,))],
        compiler_params=pltpu.CompilerParams(vmem_limit_bytes=ARRANGE_LIMIT),
        cost_estimate=pl.CostEstimate(flops=0, bytes_accessed=8 * rows * columns, transcendentals=0),
        name="arrange",
    )(starts, own, other)


def project_kernel(runs, column, count, has_total, tokens, *refs):
    pieces, outs = refs[:count], refs[count + has_total :]
    width = sum(out.shape[1] for out in outs)
    total = refs[count][:, column : column + width] if has_total else None
    for piece, row, place, depth in runs:
        part = jnp.dot(
            tokens[:, place : place + depth], pieces[piece][row : row + depth, :], preferred_element_type=jnp.float32
        )
        total = part if total is None else total + part
    first = 0
    for out in outs:
        out[...] = total[:, first : first + out.shape[1]].astype(out.dtype)
        first += out.shape[1]


def project(tokens, runs, pieces, total, column, dtype, outs):
    rows, width = tokens.shape[0], pieces[0].shape[1]
    vmem = pl.BlockSpec(memory_space=pltpu.VMEM)
    depth = sum(run[3] for run in runs)
    totals = [] if total is None else [total]
    return pl.pallas_call(
        functools.partial(project_kernel, runs, column, len(pieces), len(totals)),
        out_shape=[jax.ShapeDtypeStruct((rows, width // outs), dtype)] * outs,
        in_specs=[vmem] * (1 + len(pieces) + len(totals)),
        out_specs=[vmem] * outs,
        compiler_params=pltpu.CompilerParams(vmem_limit_bytes=PROJECT_LIMIT),
        cost_estimate=pl.CostEstimate(flops=2 * rows * depth * width, bytes_accessed=2 * rows * depth, transcendentals=0),
        name="project",
    )(tokens, *pieces, *totals)


def attend_kernel(scale, group, query_first, side_first, flag, bias, queries, held, sent, *refs):
    out_ref, key_rows, value_rows, made, sems = refs[-5:]
    is_keys = flag[:1, :] > 0
    side = slice(side_first, side_first + HEAD_WIDTH)
    key_rows[...] = jnp.where(is_keys, held[:, side], sent[:, side])
    value_rows[:, :HEAD_WIDTH] = jnp.where(is_keys, sent[:, side], held[:, side])
    value_rows[:, HEAD_WIDTH:] = jnp.ones((value_rows.shape[0], HEAD_WIDTH), jnp.bfloat16)
    step = 128
    copies = []
    for head in range(group):
        columns = slice(query_first + head * HEAD_WIDTH, query_first + (head + 1) * HEAD_WIDTH)
        for row in range(0, queries.shape[0], step):
            scores = lax.dot_general(
                queries[row : row + step, columns],
                key_rows[...],
                (((1,), (1,)), ((), ())),
                preferred_element_type=jnp.float32,
            )
            scores = scores * scale + bias[row : row + step, :]
            peak = jnp.max(scores, axis=1, keepdims=True)
            probs = jnp.exp2(scores - peak).astype(jnp.bfloat16)
            summed = jnp.dot(probs, value_rows[...], preferred_element_type=jnp.float32)
            made[head, row : row + step, :] = (summed[:, :HEAD_WIDTH] / summed[:, HEAD_WIDTH:]).astype(made.dtype)
        copies.append(pltpu.make_async_copy(made.at[head], out_ref.at[:, columns], sems.at[head]))
        copies[-1].start()
    for copy in copies:
        copy.wait()


def attend(flag, bias, queries, sides, before, head, side_head, kv_heads):
    rows, width = queries.shape
    block = width // kv_heads
    group = block // HEAD_WIDTH
    count = bias.shape[1]
    vmem = pl.BlockSpec(memory_space=pltpu.VMEM)
    anywhere = pl.BlockSpec(memory_space=pl.ANY)
    operands = [flag, bias, queries, *sides]
    in_specs = [vmem] * 5
    aliases = {}
    if before is not None:
        aliases = {len(operands): 0}
        in_specs.append(anywhere)
        operands.append(before)
    return pl.pallas_call(
        functools.partial(attend_kernel, HEAD_WIDTH**-0.5 * LOG2_E, group, head * block, side_head * HEAD_WIDTH),
        out_shape=jax.ShapeDtypeStruct((rows, width), jnp.bfloat16),
        in_specs=in_specs,
        out_specs=anywhere,
        input_output_aliases=aliases,
        scratch_shapes=[
            pltpu.VMEM((count, HEAD_WIDTH), jnp.bfloat16),
            pltpu.VMEM((count, 2 * HEAD_WIDTH), jnp.bfloat16),
            pltpu.VMEM((group, rows, HEAD_WIDTH), jnp.bfloat16),
            pltpu.SemaphoreType.DMA((group,)),
        ],
        compiler_params=pltpu.CompilerParams(vmem_limit_bytes=ATTEND_LIMIT),
        cost_estimate=pl.CostEstimate(
            flops=4 * rows * block * count,
            bytes_accessed=8 * rows * block,
            transcendentals=rows * count * block // HEAD_WIDTH,
        ),
        name="attend",
    )(*operands)


def regroup_kernel(groups, count, *refs):
    for group, out_ref in zip(groups, refs[count:]):
        place = 0
        for index, row, rows, column in group:
            out_ref[place : place + rows, :] = refs[index][row : row + rows, column : column + out_ref.shape[1]]
            place += rows


def regroup(arrays, groups, widths):
    vmem = pl.BlockSpec(memory_space=pltpu.VMEM)
    return pl.pallas_call(
        functools.partial(regroup_kernel, groups, len(arrays)),
        out_shape=[
            jax.ShapeDtypeStruct((sum(part[2] for part in group), width), arrays[0].dtype)
            for group, width in zip(groups, widths)
        ],
        in_specs=[vmem] * len(arrays),
        out_specs=[vmem] * len(groups),
        compiler_params=pltpu.CompilerParams(vmem_limit_bytes=REGROUP_LIMIT),
        cost_estimate=pl.CostEstimate(flops=0, bytes_accessed=4 * sum(array.size for array in arrays), transcendentals=0),
        name="regroup",
    )(*arrays)


def assemble_kernel(flag, mine, theirs, out_ref):
    rows = mine.shape[0]
    is_first = flag[:1, :1] > 0
    out_ref[:rows, :] = jnp.where(is_first, mine[...], theirs[...])
    out_ref[rows:, :] = jnp.where(is_first, theirs[...], mine[...])


def assemble(flag, mine, theirs):
    rows, width = mine.shape
    vmem = pl.BlockSpec(memory_space=pltpu.VMEM)
    return pl.pallas_call(
        assemble_kernel,
        out_shape=jax.ShapeDtypeStruct((2 * rows, width), mine.dtype),
        in_specs=[vmem] * 3,
        out_specs=vmem,
        compiler_params=pltpu.CompilerParams(vmem_limit_bytes=REGROUP_LIMIT),
        name="assemble",
    )(flag, mine, theirs)


def per_device(hidden, queries, layout, boundary, key_matrix, value_matrix):
    tokens, order, start_doc = hidden[0], layout[0], boundary[0]
    rows_here = tokens.shape[0]
    half = rows_here // 2
    kv_width = key_matrix.shape[1]
    kv_heads = kv_width // HEAD_WIDTH
    ctx_count, dp_count = lax.axis_size("ctx"), lax.axis_size("dp")
    here, window = lax.axis_index("ctx"), lax.axis_index("dp")
    core = here % 2
    chips = ctx_count // 2
    masks = [1 << bit for bit in range(1, ctx_count.bit_length() - 1)]

    is_keys = core == 0
    mine = jnp.where(is_keys, key_matrix, value_matrix)
    theirs = swapped(jnp.where(is_keys, value_matrix, key_matrix), 1)
    flag = jnp.broadcast_to(is_keys.astype(jnp.float32), (8, HEAD_WIDTH))
    matrix = assemble(flag, mine, theirs)
    (other_tokens, _) = lax.optimization_barrier((tokens, theirs))
    other_tokens = swapped(other_tokens, 1)

    depth = matrix.shape[0] // 2
    far_masks = [1 << bit for bit in reversed(range(dp_count.bit_length() - 1))]

    def by_plane(piece, mask):
        return swapped(piece[0], mask), [(by, xor ^ mask, part) for by, xor, part in piece[1]]

    def by_column(piece, mask):
        return across(piece[0], mask), [(by ^ mask, xor, part) for by, xor, part in piece[1]]

    def view(piece, first_name=0, count=None, start=0, columns=None):
        array, names = piece
        names = names[first_name : None if count is None else first_name + count]
        return array, first_name * depth, names, start, array.shape[1] - start if columns is None else columns

    def first(piece, **columns):
        return view(piece, 0, len(piece[1]) // 2, **columns)

    def second(piece, **columns):
        return view(piece, len(piece[1]) // 2, **columns)

    def joined(*lists):
        arrays, groups = [], []
        for views in lists:
            group = []
            for array, row, names, start, _ in views:
                index = [k for k, known in enumerate(arrays) if known is array]
                if not index:
                    arrays.append(array)
                    index = [len(arrays) - 1]
                group.append((index[0], row, len(names) * depth, start))
            groups.append(tuple(group))
        made = regroup(arrays, tuple(groups), [views[0][4] for views in lists])
        return [(rows, sum([one[2] for one in views], [])) for rows, views in zip(made, lists)]

    def nearby(piece):
        for mask in masks[2:]:
            (piece,) = joined([view(piece), view(by_plane(piece, mask))])
        return [piece, by_plane(piece, masks[0]), by_plane(piece, masks[1])]

    def onward(pieces):
        low, high = joined([first(pieces[1])], [second(pieces[2])])
        return pieces + [by_plane(low, masks[1]), by_plane(high, masks[0])]

    def along(held, mask):
        whole = held[0] if len(held) == 1 else joined([view(piece) for piece in held])[0]
        return held + [by_column(whole, mask)]

    def tied(values, *others):
        arrays = [value[0] if isinstance(value, tuple) else value for value in values]
        after = lax.optimization_barrier((*arrays, *others))
        return [(array, value[1]) if isinstance(value, tuple) else array for array, value in zip(after, values)]

    plane = list(range(2, ctx_count, 2))

    def sent_round(made):
        return [made] + [swapped(made, xor) for xor in plane]

    def both_sides(parts):
        rows, width = parts[0].shape
        (held,) = regroup(parts, (tuple((index, 0, rows, 0) for index in range(len(parts))),), [width])
        return held, swapped(held, 1)

    sources = [(here // 2 * 2 ^ xor) + side for xor in [0] + plane for side in range(2)]
    block_ids = jnp.arange(order.shape[0], dtype=jnp.int32)

    def positions(devices):
        blocks = (jnp.stack(devices)[:, None] * 2 + jnp.arange(2)[None, :]).reshape(-1)
        looked = jnp.sum(jnp.where(blocks[:, None] == block_ids[None, :], order[None, :], 0), axis=1)
        return (looked[:, None] * half + jnp.arange(half, dtype=jnp.int32)[None, :]).reshape(-1)

    query_pos = positions([here])[:, None]
    key_pos = positions(sources)[None, :]
    allowed = (key_pos <= query_pos) & ((key_pos >= start_doc) | (query_pos < start_doc))
    bias = jnp.where(allowed, 0.0, -jnp.inf).astype(jnp.float32)

    cuts = [(0, 1), (1, kv_heads - 2), (kv_heads - 1, 1)]

    def cut(index):
        start, count = cuts[index]
        return {"start": start * HEAD_WIDTH, "columns": count * HEAD_WIDTH}

    column = [0]
    for mask in far_masks:
        column = column + [by ^ mask for by in column]
    plane_xors = [0, masks[0], masks[1], masks[0] ^ masks[1]]
    for mask in masks[2:]:
        plane_xors = plane_xors + [xor ^ mask for xor in plane_xors]
    own_order = [(0, xor, part) for xor in plane_xors for part in range(2)]
    order_of = own_order + [(by, xor, part) for xor in plane_xors for part in range(2) for by in column[1:]]
    starts = [((window ^ by) * chips + ((here ^ xor) // 2)) * 2 + part for by, xor, part in order_of]
    ordered = depth % 128 == 0
    if ordered:
        arranged = arrange(jnp.stack([core, *starts]).astype(jnp.int32), tokens, other_tokens)
    else:
        both = jnp.where(is_keys, 0, 1)
        arranged = jnp.stack((tokens, other_tokens))[jnp.stack((both, 1 - both))].reshape(2 * rows_here, -1)
        arranged = jnp.take(arranged.reshape(2 * rows_here, -1, depth), jnp.stack(starts), axis=1)
        arranged = arranged.reshape(2 * rows_here, -1)

    def project_pieces(pieces, total, start, dtype):
        runs = []
        for index, (_, names) in enumerate(pieces):
            for block, name in enumerate(names):
                row, place = block * depth, order_of.index(name) * depth
                if runs and runs[-1][0] == index and runs[-1][2] + runs[-1][3] == place:
                    runs[-1] = (*runs[-1][:3], runs[-1][3] + depth)
                else:
                    runs.append((index, row, place, depth))
        return project(arranged, tuple(runs), [rows for rows, _ in pieces], total, start * HEAD_WIDTH, dtype, 1)

    def project_cut(index, pieces):
        return project_pieces(pieces, own_total, cuts[index][0], jnp.bfloat16)

    def attend_head(head, held, result, side_head=0):
        return attend(flag, bias, queries[0], held, result, head, side_head, kv_heads)

    mine_rows = (matrix, [(0, 0, 0), (0, 0, 1)])
    own = nearby(mine_rows)
    column_a = along(joined([view(mine_rows, **cut(0))]), far_masks[0])
    for mask in far_masks[1:]:
        column_a = along(column_a, mask)

    def halves(index):
        low = [first(own[0], **cut(index)), first(own[1], **cut(index))]
        high = [second(own[0], **cut(index)), second(own[2], **cut(index))]
        return low + high

    (start_b,) = tied(joined([view(mine_rows, **cut(1))]), column_a[-1][0])
    column_b = along([start_b], far_masks[0])
    all_own = onward(own)

    def sorted_views(held, places):
        size = len(held[0][1])
        part = size // places
        views = [[] for _ in range(places)]
        for piece in held[1:]:
            for block in range(0, len(piece[1]), size):
                for place in range(places):
                    views[place].append(view(piece, block + place * part, part))
        return views

    (rest_a,) = joined(sum(sorted_views(column_a, 2), []))
    near_a = nearby(rest_a)

    def last_exchange(held):
        views = sorted_views(held, 4)
        low, high = joined(views[0] + views[1], views[2] + views[3])
        return [low, high, by_plane(low, masks[1]), by_plane(high, masks[0])]

    tick = tied([arranged, *near_a, *all_own, *column_b])
    arranged, near_a, all_own, column_b = tick[0], tick[1:4], tick[4:9], tick[9:]
    all_a = onward(near_a)
    for mask in far_masks[1:]:
        column_b = along(column_b, mask)
    (own_total,) = project_pieces(all_own, None, 0, jnp.float32)

    tick = tied([own_total, *all_a])
    own_total, all_a = tick[0], tick[1:]
    (made_a,) = project_cut(0, all_a)
    parts_a = sent_round(made_a)
    (rest_b,) = joined(sum(sorted_views(column_b, 2), []))
    near_b = nearby(rest_b)
    (start_c,) = tied(joined(halves(2)), column_b[-1][0])
    column_c = [start_c]
    for mask in far_masks:
        column_c = along(column_c, mask)
    result = attend_head(0, both_sides(parts_a), None)

    tick = tied([result, *near_b, *column_c])
    result, near_b, column_c = tick[0], tick[1:4], tick[4:]
    all_b = onward(near_b)
    all_c = last_exchange(column_c)
    (part_b,) = project_pieces(all_b[:3], own_total, cuts[1][0], jnp.float32)
    part_b, *last_b = tied([part_b, *all_b[3:]])
    (made_b,) = project_pieces(last_b, part_b, 0, jnp.bfloat16)

    parts_b = sent_round(made_b)
    (part_c,) = project_pieces(all_c[:2], own_total, cuts[2][0], jnp.float32)
    part_c, parts_b[0], *last_c = tied([part_c, parts_b[0], *all_c[2:]])
    (made_c,) = project_pieces(last_c, part_c, 0, jnp.bfloat16)
    parts_c = sent_round(made_c)
    tick = tied([*parts_b, parts_c[0]])
    parts_b, parts_c[0] = tick[:-1], tick[-1]
    side_b = both_sides(parts_b)
    count = cuts[1][1]
    for head in range(count):
        if head == count - 1:
            result, *parts_c = tied([result, *parts_c])
            side_c = both_sides(parts_c)
        result = attend_head(1 + head, side_b, result, head)
    result = attend_head(kv_heads - 1, side_c, result)
    return result[None]


def solution(mesh):
    in_specs = (
        P("dp", "ctx", None),
        P("dp", "ctx", None),
        P("dp", None),
        P("dp"),
        P(("dp", "ctx"), None),
        P(("dp", "ctx"), None),
    )
    out_specs = P("dp", "ctx", None)
    return jax.shard_map(
        per_device, mesh=mesh, in_specs=in_specs, out_specs=out_specs, check_vma=False
    )
```

time: 138 us -> 136 us (0.986)
  Pallas kernels: 39.7 us -> 41.5 us
  other arithmetic: 4.02 us -> 2.29 us
    ppermute x30 -> x28, waiting for transfers between devices: 44.7 us -> 24.8 us  [swapped(): return lax.ppermute(value, 'ctx', [(i, i ^ mask) for i in range(size)])]
    ppermute x6, waiting for transfers between devices: 4.02 us -> 23.6 us  [across(): return lax.ppermute(value, 'dp', [(i, i ^ mask) for i in range(size)])]
    ppermute x30 -> x28, starting transfers between devices: 30.7 us -> 27.7 us  [swapped(): return lax.ppermute(value, 'ctx', [(i, i ^ mask) for i in range(size)])]
    pallas_call x4 -> x22, Pallas kernels: 6.8 us -> 9.33 us  [the longest x6 7.88 us: project(): pl.pallas_call(functools.partial(project_kernel, runs, column, len(pieces...]
    ppermute x6, starting transfers between devices: 10.5 us -> 12.3 us  [across(): return lax.ppermute(value, 'dp', [(i, i ^ mask) for i in range(size)])]
  transfers between devices with their start and end apart: 36 -> 34, of which waited for: 21 -> 16; matrix products, arithmetic and copies ran while one was open for 3% -> 1% of each run, Pallas kernels for 24% -> 25%
where the time goes in v1:
time: 136 us
  waiting for transfers between devices  48.5 us (36%)
  Pallas kernels  41.5 us (31%)
  starting transfers between devices  40 us (29%)
  local copies, waits for them, and re-layouts  2.48 us (2%)
  other arithmetic  2.29 us (2%)
    pallas_call x4, Pallas kernels, attend(): pl.pallas_call(functools.partial(attend_kernel, HEAD_WIDTH ** (-0.5) * LO...  28 us
    ppermute x28, starting transfers between devices, swapped(): return lax.ppermute(value, 'ctx', [(i, i ^ mask) for i in range(size)])  27.7 us
    ppermute x28, waiting for transfers between devices, swapped(): return lax.ppermute(value, 'ctx', [(i, i ^ mask) for i in range(size)])  24.8 us
    ppermute x6, waiting for transfers between devices, across(): return lax.ppermute(value, 'dp', [(i, i ^ mask) for i in range(size)])  23.6 us
    ppermute x6, starting transfers between devices, across(): return lax.ppermute(value, 'dp', [(i, i ^ mask) for i in range(size)])  12.3 us
    pallas_call x6, Pallas kernels, project(): pl.pallas_call(functools.partial(project_kernel, runs, column, len(pieces...  7.88 us
    pallas_call x1, Pallas kernels, arrange(): pl.pallas_call(functools.partial(arrange_kernel, blocks), out_shape=jax.S...  4.19 us
  transfers between devices with their start and end apart: 34, of which 16 were waited for; matrix products, arithmetic and copies ran while one was open for 1% of the time, Pallas kernels for 25%

profile of v1, /device:TPU:0, one launch (start us, length us, event | category | flops | bytes accessed | tf_op | source)
XLA Modules:
  0.0 136.0 jit_solution(12483900162217286019)
XLA Ops:
  3.4 2.7 %collective-permute-start.6 = (bf16[512,512]{1,0:T(8,128)(2,1)S(1)}, bf16[512,512]{1,0:T(8,128)(2,1)S(1)}, u32[]{:S(2)}, u32[]{:S(2)}) collective-permute-start(bf16[512,512]{1,0:T(8,128)(2,1)S(1)} %assemble.1.refs_0_), channel_id=1, source_target_pairs={{0,2},{1,3},{2,0},{3,1},{4,6},{5,7},{6,4},{7,5},{8,10},{9,11},{10,... | collective-permute-start | bytes 1572872 | tf_op jit(solution)/shard_map/ppermute | solution.py:20
  6.1 1.5 %collective-permute-start.7 = (bf16[512,512]{1,0:T(8,128)(2,1)S(1)}, bf16[512,512]{1,0:T(8,128)(2,1)S(1)}, u32[]{:S(2)}, u32[]{:S(2)}) collective-permute-start(bf16[512,512]{1,0:T(8,128)(2,1)S(1)} %assemble.1.refs_0_), channel_id=1, source_target_pairs={{0,4},{1,5},{2,6},{3,7},{4,0},{5,1},{6,2},{7,3},{8,12},{9,13},{10,... | collective-permute-start | bytes 1572872 | tf_op jit(solution)/shard_map/ppermute | solution.py:20
  7.6 2.6 %collective-permute-start.2 = (bf16[512,128]{1,0:T(8,128)(2,1)S(1)}, bf16[512,128]{1,0:T(8,128)(2,1)S(1)}, u32[]{:S(2)}, u32[]{:S(2)}) collective-permute-start(bf16[512,128]{1,0:T(8,128)(2,1)S(1)} %regroup.15.refs_0_), channel_id=1, source_target_pairs={{0,16},{8,24},{16,0},{24,8},{1,17},{9,25},{17,1},{25,9},{2,18},{10... | collective-permute-start | bytes 393224 | tf_op jit(solution)/shard_map/ppermute | solution.py:25
  10.3 6.2 %collective-permute-done.2.refs_1_.refs_0_ = bf16[512,128]{1,0:T(8,128)(2,1)S(1)} collective-permute-done((bf16[512,128]{1,0:T(8,128)(2,1)S(1)}, bf16[512,128]{1,0:T(8,128)(2,1)S(1)}, u32[]{:S(2)}, u32[]{:S(2)}) %collective-permute-start.2) | collective-permute-done | bytes 131104 | tf_op jit(solution)/shard_map/ppermute | solution.py:25
  18.1 5.6 %collective-permute-done.3.refs_1_ = bf16[1024,128]{1,0:T(8,128)(2,1)S(1)} collective-permute-done((bf16[1024,128]{1,0:T(8,128)(2,1)S(1)}, bf16[1024,128]{1,0:T(8,128)(2,1)S(1)}, u32[]{:S(2)}, u32[]{:S(2)}) %collective-permute-start.3) | collective-permute-done | bytes 262176 | tf_op jit(solution)/shard_map/ppermute | solution.py:25
  25.1 3.1 %collective-permute-start.10 = (bf16[512,256]{1,0:T(8,128)(2,1)S(1)}, bf16[512,256]{1,0:T(8,128)(2,1)S(1)}, u32[]{:S(2)}, u32[]{:S(2)}) collective-permute-start(bf16[512,256]{1,0:T(8,128)(2,1)S(1)} %regroup.19.refs_0_), channel_id=1, source_target_pairs={{0,16},{8,24},{16,0},{24,8},{1,17},{9,25},{17,1},{25,9},{2,18},{10... | collective-permute-start | bytes 786440 | tf_op jit(solution)/shard_map/ppermute | solution.py:25
  29.1 1.5 %collective-permute-start.8 = (bf16[256,512]{1,0:T(8,128)(2,1)}, bf16[256,512]{1,0:T(8,128)(2,1)S(1)}, u32[]{:S(2)}, u32[]{:S(2)}) collective-permute-start(bf16[256,512]{1,0:T(8,128)(2,1)} %get-tuple-element.57), channel_id=1, source_target_pairs={{0,4},{1,5},{2,6},{3,7},{4,0},{5,1},{6,2},{7,3},{8,12},{9,13},{10,... | collective-permute-start | bytes 786440 | tf_op jit(solution)/shard_map/ppermute | solution.py:20
  30.6 1.5 %collective-permute-start.9 = (bf16[256,512]{1,0:T(8,128)(2,1)}, bf16[256,512]{1,0:T(8,128)(2,1)}, u32[]{:S(2)}, u32[]{:S(2)}) collective-permute-start(bf16[256,512]{1,0:T(8,128)(2,1)} %get-tuple-element.58), channel_id=1, source_target_pairs={{0,2},{1,3},{2,0},{3,1},{4,6},{5,7},{6,4},{7,5},{8,10},{9,11},{10,... | collective-permute-start | bytes 786440 | tf_op jit(solution)/shard_map/ppermute | solution.py:20
  32.4 2.2 %copy-done.1 = bf16[1,256,8192]{2,1,0:T(8,128)(2,1)S(1)} copy-done((bf16[1,256,8192]{2,1,0:T(8,128)(2,1)S(1)}, bf16[1,256,8192]{2,1,0:T(8,128)(2,1)}, u32[]{:S(2)}) %copy-start.1) | copy-done | bytes 4194328
  34.6 4.2 %arrange.1.tokens = bf16[512,8192]{1,0:T(8,128)(2,1)S(1)} custom-call(s32[33]{0:T(128)S(1)} %stack.171.starts, bf16[256,8192]{1,0:T(8,128)(2,1)S(1)} %bitcast.61, bf16[256,8192]{1,0:T(8,128)(2,1)} %collective-permute-done.1.other_ref), custom_call_target="tpu_custom_call" | custom-call | bytes 16777216 | tf_op jit(solution)/shard_map/arrange/pallas_call | solution.py:53
  39.3 2.4 %collective-permute-start.17 = (bf16[1024,256]{1,0:T(8,128)(2,1)S(1)}, bf16[1024,256]{1,0:T(8,128)(2,1)S(1)}, u32[]{:S(2)}, u32[]{:S(2)}) collective-permute-start(bf16[1024,256]{1,0:T(8,128)(2,1)S(1)} %regroup.22), channel_id=1, source_target_pairs={{0,8},{8,0},{16,24},{24,16},{1,9},{9,1},{17,25},{25,17},{2,10},{10... | collective-permute-start | bytes 1572872 | tf_op jit(solution)/shard_map/ppermute | solution.py:25
  42.5 1.5 %collective-permute-start.12 = (bf16[768,128]{1,0:T(8,128)(2,1)S(1)}, bf16[768,128]{1,0:T(8,128)(2,1)S(1)}, u32[]{:S(2)}, u32[]{:S(2)}) collective-permute-start(bf16[768,128]{1,0:T(8,128)(2,1)S(1)} %get-tuple-element.70), channel_id=1, source_target_pairs={{0,2},{1,3},{2,0},{3,1},{4,6},{5,7},{6,4},{7,5},{8,10},{9,11},{10,... | collective-permute-start | bytes 589832 | tf_op jit(solution)/shard_map/ppermute | solution.py:20
  44.1 2.2 %project.6.refs_5_.refs_2_.refs_3_ = f32[512,512]{1,0:T(8,128)S(1)} custom-call(bf16[512,8192]{1,0:T(8,128)(2,1)S(1)} %arrange.1.tokens, bf16[512,512]{1,0:T(8,128)(2,1)S(1)} %assemble.1.refs_0_, bf16[512,512]{1,0:T(8,128)(2,1)S(1)} %collective-permute-done.6.refs_0_.refs_1_, bf16[512,512]{1,0:T(8,128)(2,1)S(1)} %collective-permute-done.7.refs_1_.refs_2_, ...), custom_call_target="tpu_custom_call" | custom-call | flops 1073741824 | bytes 2097152 | tf_op jit(solution)/shard_map/project/pallas_call | solution.py:85
  48.2 1.8 %project.7.refs_0_ = bf16[512,128]{1,0:T(8,128)(2,1)S(1)} custom-call(bf16[512,8192]{1,0:T(8,128)(2,1)S(1)} %arrange.1.tokens, bf16[1536,128]{1,0:T(8,128)(2,1)S(1)} %regroup.17.refs_0_, bf16[1536,128]{1,0:T(8,128)(2,1)S(1)} %collective-permute-done.4.refs_0_.refs_1_, bf16[1536,128]{1,0:T(8,128)(2,1)S(1)} %collective-permute-done.5.refs_1_.refs_2_, ...), custom_call_target="tpu_custom_call" | custom-call | flops 805306368 | bytes 6291456 | tf_op jit(solution)/shard_map/project/pallas_call | solution.py:85
  50.0 1.6 %collective-permute-start.13 = (bf16[512,128]{1,0:T(8,128)(2,1)S(1)}, bf16[512,128]{1,0:T(8,128)(2,1)S(1)}, u32[]{:S(2)}, u32[]{:S(2)}) collective-permute-start(bf16[512,128]{1,0:T(8,128)(2,1)S(1)} %project.7.refs_0_), channel_id=1, source_target_pairs={{0,2},{1,3},{2,0},{3,1},{4,6},{5,7},{6,4},{7,5},{8,10},{9,11},{10,... | collective-permute-start | bytes 393224 | tf_op jit(solution)/shard_map/ppermute | solution.py:20
  51.6 1.5 %collective-permute-start.14 = (bf16[512,128]{1,0:T(8,128)(2,1)S(1)}, bf16[512,128]{1,0:T(8,128)(2,1)S(1)}, u32[]{:S(2)}, u32[]{:S(2)}) collective-permute-start(bf16[512,128]{1,0:T(8,128)(2,1)S(1)} %project.7.refs_0_), channel_id=1, source_target_pairs={{0,4},{1,5},{2,6},{3,7},{4,0},{5,1},{6,2},{7,3},{8,12},{9,13},{10,... | collective-permute-start | bytes 393224 | tf_op jit(solution)/shard_map/ppermute | solution.py:20
  53.6 3.4 %collective-permute-start.20 = (bf16[1024,128]{1,0:T(8,128)(2,1)S(1)}, bf16[1024,128]{1,0:T(8,128)(2,1)S(1)}, u32[]{:S(2)}, u32[]{:S(2)}) collective-permute-start(bf16[1024,128]{1,0:T(8,128)(2,1)S(1)} %regroup.24.refs_0_), channel_id=1, source_target_pairs={{0,16},{8,24},{16,0},{24,8},{1,17},{9,25},{17,1},{25,9},{2,18},{10... | collective-permute-start | bytes 786440 | tf_op jit(solution)/shard_map/ppermute | solution.py:25
  57.0 1.9 %collective-permute-done.15.refs_3_ = bf16[512,128]{1,0:T(8,128)(2,1)S(1)} collective-permute-done((bf16[512,128]{1,0:T(8,128)(2,1)S(1)}, bf16[512,128]{1,0:T(8,128)(2,1)S(1)}, u32[]{:S(2)}, u32[]{:S(2)}) %collective-permute-start.15) | collective-permute-done | bytes 131104 | tf_op jit(solution)/shard_map/ppermute | solution.py:20
  60.4 5.7 %collective-permute-done.20.refs_1_.refs_0_ = bf16[1024,128]{1,0:T(8,128)(2,1)S(1)} collective-permute-done((bf16[1024,128]{1,0:T(8,128)(2,1)S(1)}, bf16[1024,128]{1,0:T(8,128)(2,1)S(1)}, u32[]{:S(2)}, u32[]{:S(2)}) %collective-permute-start.20) | collective-permute-done | bytes 262176 | tf_op jit(solution)/shard_map/ppermute | solution.py:25
  66.7 6.9 %attend.4.refs_0_ = bf16[256,4096]{1,0:T(8,128)(2,1)} custom-call(f32[8,128]{1,0:T(8,128)S(1)} %broadcast_in_dim.49.flag, f32[256,2048]{1,0:T(8,128)S(1)} %and_select_fusion.bias, bf16[256,4096]{1,0:T(8,128)(2,1)S(1)} %bitcast.56, bf16[2048,128]{1,0:T(8,128)(2,1)S(1)} %regroup.21.held, bf16[2048,128]{1,0:T(8,128)(2,1)S(1)} %collective-permute-done.16.sent), custom_call_target="tpu_custom_call" | custom-call | flops 2147483648 | bytes 2097152 | tf_op jit(solution)/shard_map/attend/pallas_call | solution.py:139
  73.7 5.6 %collective-permute-done.21.refs_1_ = bf16[2048,128]{1,0:T(8,128)(2,1)S(1)} collective-permute-done((bf16[2048,128]{1,0:T(8,128)(2,1)S(1)}, bf16[2048,128]{1,0:T(8,128)(2,1)S(1)}, u32[]{:S(2)}, u32[]{:S(2)}) %collective-permute-start.21) | collective-permute-done | bytes 524320 | tf_op jit(solution)/shard_map/ppermute | solution.py:25
  81.6 1.6 %collective-permute-start.24 = (bf16[1536,128]{1,0:T(8,128)(2,1)S(1)}, bf16[1536,128]{1,0:T(8,128)(2,1)S(1)}, u32[]{:S(2)}, u32[]{:S(2)}) collective-permute-start(bf16[1536,128]{1,0:T(8,128)(2,1)S(1)} %get-tuple-element.82.refs_0_), channel_id=1, source_target_pairs={{0,4},{1,5},{2,6},{3,7},{4,0},{5,1},{6,2},{7,3},{8,12},{9,13},{10,... | collective-permute-start | bytes 1179656 | tf_op jit(solution)/shard_map/ppermute | solution.py:20
  85.1 6.5 %collective-permute-done.22.refs_0_ = bf16[768,256]{1,0:T(8,128)(2,1)S(1)} collective-permute-done((bf16[768,256]{1,0:T(8,128)(2,1)S(1)}, bf16[768,256]{1,0:T(8,128)(2,1)S(1)}, u32[]{:S(2)}, u32[]{:S(2)}) %collective-permute-start.22) | collective-permute-done | bytes 393248 | tf_op jit(solution)/shard_map/ppermute | solution.py:20
  92.7 1.5 %collective-permute-start.26 = (bf16[512,256]{1,0:T(8,128)(2,1)S(1)}, bf16[512,256]{1,0:T(8,128)(2,1)S(1)}, u32[]{:S(2)}, u32[]{:S(2)}) collective-permute-start(bf16[512,256]{1,0:T(8,128)(2,1)S(1)} %project.10.refs_0_), channel_id=1, source_target_pairs={{0,2},{1,3},{2,0},{3,1},{4,6},{5,7},{6,4},{7,5},{8,10},{9,11},{10,... | collective-permute-start | bytes 786440 | tf_op jit(solution)/shard_map/ppermute | solution.py:20
  94.2 1.5 %collective-permute-start.27 = (bf16[512,256]{1,0:T(8,128)(2,1)S(1)}, bf16[512,256]{1,0:T(8,128)(2,1)S(1)}, u32[]{:S(2)}, u32[]{:S(2)}) collective-permute-start(bf16[512,256]{1,0:T(8,128)(2,1)S(1)} %project.10.refs_0_), channel_id=1, source_target_pairs={{0,4},{1,5},{2,6},{3,7},{4,0},{5,1},{6,2},{7,3},{8,12},{9,13},{10,... | collective-permute-start | bytes 786440 | tf_op jit(solution)/shard_map/ppermute | solution.py:20
  97.2 2.8 %collective-permute-done.24.refs_0_ = bf16[1536,128]{1,0:T(8,128)(2,1)S(1)} collective-permute-done((bf16[1536,128]{1,0:T(8,128)(2,1)S(1)}, bf16[1536,128]{1,0:T(8,128)(2,1)S(1)}, u32[]{:S(2)}, u32[]{:S(2)}) %collective-permute-start.24) | collective-permute-done | bytes 393248 | tf_op jit(solution)/shard_map/ppermute | solution.py:20
  101.5 4.6 %collective-permute-done.26.refs_1_ = bf16[512,256]{1,0:T(8,128)(2,1)S(1)} collective-permute-done((bf16[512,256]{1,0:T(8,128)(2,1)S(1)}, bf16[512,256]{1,0:T(8,128)(2,1)S(1)}, u32[]{:S(2)}, u32[]{:S(2)}) %collective-permute-start.26) | collective-permute-done | bytes 262176 | tf_op jit(solution)/shard_map/ppermute | solution.py:20
  106.2 4.7 %collective-permute-done.28.refs_3_ = bf16[512,256]{1,0:T(8,128)(2,1)S(1)} collective-permute-done((bf16[512,256]{1,0:T(8,128)(2,1)S(1)}, bf16[512,256]{1,0:T(8,128)(2,1)S(1)}, u32[]{:S(2)}, u32[]{:S(2)}) %collective-permute-start.28) | collective-permute-done | bytes 262176 | tf_op jit(solution)/shard_map/ppermute | solution.py:20
  113.0 1.6 %collective-permute-start.32 = (bf16[512,128]{1,0:T(8,128)(2,1)S(1)}, bf16[512,128]{1,0:T(8,128)(2,1)S(1)}, u32[]{:S(2)}, u32[]{:S(2)}) collective-permute-start(bf16[512,128]{1,0:T(8,128)(2,1)S(1)} %project.11.refs_0_), channel_id=1, source_target_pairs={{0,6},{1,7},{2,4},{3,5},{4,2},{5,3},{6,0},{7,1},{8,14},{9,15},{10,... | collective-permute-start | bytes 393224 | tf_op jit(solution)/shard_map/ppermute | solution.py:20
  114.6 6.9 %attend.5.refs_0_ = bf16[256,4096]{1,0:T(8,128)(2,1)} custom-call(f32[8,128]{1,0:T(8,128)S(1)} %broadcast_in_dim.49.flag, f32[256,2048]{1,0:T(8,128)S(1)} %and_select_fusion.bias, bf16[256,4096]{1,0:T(8,128)(2,1)S(1)} %bitcast.57, bf16[2048,256]{1,0:T(8,128)(2,1)S(1)} %regroup.28.held, ...), custom_call_target="tpu_custom_call", output_to_operand_aliasing={{}: (5, {})} | custom-call | flops 2147483648 | bytes 2097152 | tf_op jit(solution)/shard_map/attend/pallas_call | solution.py:139
  121.6 7.2 %attend.6.refs_0_ = bf16[256,4096]{1,0:T(8,128)(2,1)} custom-call(f32[8,128]{1,0:T(8,128)S(1)} %broadcast_in_dim.49.flag, f32[256,2048]{1,0:T(8,128)S(1)} %and_select_fusion.bias, bf16[256,4096]{1,0:T(8,128)(2,1)S(1)} %bitcast.58, bf16[2048,256]{1,0:T(8,128)(2,1)S(1)} %regroup.28.held, ...), custom_call_target="tpu_custom_call", output_to_operand_aliasing={{}: (5, {})} | custom-call | flops 2147483648 | bytes 2097152 | tf_op jit(solution)/shard_map/attend/pallas_call | solution.py:139
  128.8 7.0 %attend.7 = bf16[256,4096]{1,0:T(8,128)(2,1)} custom-call(f32[8,128]{1,0:T(8,128)S(1)} %broadcast_in_dim.49.flag, f32[256,2048]{1,0:T(8,128)S(1)} %and_select_fusion.bias, bf16[256,4096]{1,0:T(8,128)(2,1)S(1)} %bitcast.59, bf16[2048,128]{1,0:T(8,128)(2,1)S(1)} %regroup.29.held, ...), custom_call_target="tpu_custom_call", output_to_operand_aliasing={{}: (5, {})} | custom-call | flops 2147483648 | bytes 2097152 | tf_op jit(solution)/shard_map/attend/pallas_call | solution.py:139
  (88 shorter events, 23.3 us)
Async XLA Ops:
  2.8 27.9 %collective-permute-start.1 = (bf16[256,8192]{1,0:T(8,128)(2,1)}, bf16[256,8192]{1,0:T(8,128)(2,1)}, u32[]{:S(2)}, u32[]{:S(2)}) collective-permute-start(bf16[256,8192]{1,0:T(8,128)(2,1)} %bitcast.60), channel_id=1, source_target_pairs={{0,1},{1,0},{2,3},{3,2},{4,5},{5,4},{6,7},{7,6},{8,9},{9,8},{10,11... | collective-permute-start | bytes 12582920 | tf_op jit(solution)/shard_map/ppermute | solution.py:20
  3.4 21.8 %collective-permute-start.6 = (bf16[512,512]{1,0:T(8,128)(2,1)S(1)}, bf16[512,512]{1,0:T(8,128)(2,1)S(1)}, u32[]{:S(2)}, u32[]{:S(2)}) collective-permute-start(bf16[512,512]{1,0:T(8,128)(2,1)S(1)} %assemble.1.refs_0_), channel_id=1, source_target_pairs={{0,2},{1,3},{2,0},{3,1},{4,6},{5,7},{6,4},{7,5},{8,10},{9,11},{10,... | collective-permute-start | bytes 1572872 | tf_op jit(solution)/shard_map/ppermute | solution.py:20
  6.1 22.2 %collective-permute-start.7 = (bf16[512,512]{1,0:T(8,128)(2,1)S(1)}, bf16[512,512]{1,0:T(8,128)(2,1)S(1)}, u32[]{:S(2)}, u32[]{:S(2)}) collective-permute-start(bf16[512,512]{1,0:T(8,128)(2,1)S(1)} %assemble.1.refs_0_), channel_id=1, source_target_pairs={{0,4},{1,5},{2,6},{3,7},{4,0},{5,1},{6,2},{7,3},{8,12},{9,13},{10,... | collective-permute-start | bytes 1572872 | tf_op jit(solution)/shard_map/ppermute | solution.py:20
  7.6 8.9 %collective-permute-start.2 = (bf16[512,128]{1,0:T(8,128)(2,1)S(1)}, bf16[512,128]{1,0:T(8,128)(2,1)S(1)}, u32[]{:S(2)}, u32[]{:S(2)}) collective-permute-start(bf16[512,128]{1,0:T(8,128)(2,1)S(1)} %regroup.15.refs_0_), channel_id=1, source_target_pairs={{0,16},{8,24},{16,0},{24,8},{1,17},{9,25},{17,1},{25,9},{2,18},{10... | collective-permute-start | bytes 393224 | tf_op jit(solution)/shard_map/ppermute | solution.py:25
  16.5 7.3 %collective-permute-start.3 = (bf16[1024,128]{1,0:T(8,128)(2,1)S(1)}, bf16[1024,128]{1,0:T(8,128)(2,1)S(1)}, u32[]{:S(2)}, u32[]{:S(2)}) collective-permute-start(bf16[1024,128]{1,0:T(8,128)(2,1)S(1)} %regroup.16), channel_id=1, source_target_pairs={{0,8},{8,0},{16,24},{24,16},{1,9},{9,1},{17,25},{25,17},{2,10},{10... | collective-permute-start | bytes 786440 | tf_op jit(solution)/shard_map/ppermute | solution.py:25
  23.8 15.5 %collective-permute-start.4 = (bf16[1536,128]{1,0:T(8,128)(2,1)S(1)}, bf16[1536,128]{1,0:T(8,128)(2,1)S(1)}, u32[]{:S(2)}, u32[]{:S(2)}) collective-permute-start(bf16[1536,128]{1,0:T(8,128)(2,1)S(1)} %regroup.17.refs_0_), channel_id=1, source_target_pairs={{0,2},{1,3},{2,0},{3,1},{4,6},{5,7},{6,4},{7,5},{8,10},{9,11},{10,... | collective-permute-start | bytes 1179656 | tf_op jit(solution)/shard_map/ppermute | solution.py:20
  24.4 14.9 %collective-permute-start.5 = (bf16[1536,128]{1,0:T(8,128)(2,1)S(1)}, bf16[1536,128]{1,0:T(8,128)(2,1)S(1)}, u32[]{:S(2)}, u32[]{:S(2)}) collective-permute-start(bf16[1536,128]{1,0:T(8,128)(2,1)S(1)} %regroup.17.refs_0_), channel_id=1, source_target_pairs={{0,4},{1,5},{2,6},{3,7},{4,0},{5,1},{6,2},{7,3},{8,12},{9,13},{10,... | collective-permute-start | bytes 1179656 | tf_op jit(solution)/shard_map/ppermute | solution.py:20
  25.1 14.2 %collective-permute-start.10 = (bf16[512,256]{1,0:T(8,128)(2,1)S(1)}, bf16[512,256]{1,0:T(8,128)(2,1)S(1)}, u32[]{:S(2)}, u32[]{:S(2)}) collective-permute-start(bf16[512,256]{1,0:T(8,128)(2,1)S(1)} %regroup.19.refs_0_), channel_id=1, source_target_pairs={{0,16},{8,24},{16,0},{24,8},{1,17},{9,25},{17,1},{25,9},{2,18},{10... | collective-permute-start | bytes 786440 | tf_op jit(solution)/shard_map/ppermute | solution.py:25
  29.1 10.2 %collective-permute-start.8 = (bf16[256,512]{1,0:T(8,128)(2,1)}, bf16[256,512]{1,0:T(8,128)(2,1)S(1)}, u32[]{:S(2)}, u32[]{:S(2)}) collective-permute-start(bf16[256,512]{1,0:T(8,128)(2,1)} %get-tuple-element.57), channel_id=1, source_target_pairs={{0,4},{1,5},{2,6},{3,7},{4,0},{5,1},{6,2},{7,3},{8,12},{9,13},{10,... | collective-permute-start | bytes 786440 | tf_op jit(solution)/shard_map/ppermute | solution.py:20
  30.6 8.7 %collective-permute-start.9 = (bf16[256,512]{1,0:T(8,128)(2,1)}, bf16[256,512]{1,0:T(8,128)(2,1)}, u32[]{:S(2)}, u32[]{:S(2)}) collective-permute-start(bf16[256,512]{1,0:T(8,128)(2,1)} %get-tuple-element.58), channel_id=1, source_target_pairs={{0,2},{1,3},{2,0},{3,1},{4,6},{5,7},{6,4},{7,5},{8,10},{9,11},{10,... | collective-permute-start | bytes 786440 | tf_op jit(solution)/shard_map/ppermute | solution.py:20
  39.3 14.2 %collective-permute-start.17 = (bf16[1024,256]{1,0:T(8,128)(2,1)S(1)}, bf16[1024,256]{1,0:T(8,128)(2,1)S(1)}, u32[]{:S(2)}, u32[]{:S(2)}) collective-permute-start(bf16[1024,256]{1,0:T(8,128)(2,1)S(1)} %regroup.22), channel_id=1, source_target_pairs={{0,8},{8,0},{16,24},{24,16},{1,9},{9,1},{17,25},{25,17},{2,10},{10... | collective-permute-start | bytes 1572872 | tf_op jit(solution)/shard_map/ppermute | solution.py:25
  42.0 5.7 %collective-permute-start.11 = (bf16[768,128]{1,0:T(8,128)(2,1)S(1)}, bf16[768,128]{1,0:T(8,128)(2,1)S(1)}, u32[]{:S(2)}, u32[]{:S(2)}) collective-permute-start(bf16[768,128]{1,0:T(8,128)(2,1)S(1)} %get-tuple-element.69), channel_id=1, source_target_pairs={{0,4},{1,5},{2,6},{3,7},{4,0},{5,1},{6,2},{7,3},{8,12},{9,13},{10,... | collective-permute-start | bytes 589832 | tf_op jit(solution)/shard_map/ppermute | solution.py:20
  42.5 5.7 %collective-permute-start.12 = (bf16[768,128]{1,0:T(8,128)(2,1)S(1)}, bf16[768,128]{1,0:T(8,128)(2,1)S(1)}, u32[]{:S(2)}, u32[]{:S(2)}) collective-permute-start(bf16[768,128]{1,0:T(8,128)(2,1)S(1)} %get-tuple-element.70), channel_id=1, source_target_pairs={{0,2},{1,3},{2,0},{3,1},{4,6},{5,7},{6,4},{7,5},{8,10},{9,11},{10,... | collective-permute-start | bytes 589832 | tf_op jit(solution)/shard_map/ppermute | solution.py:20
  50.0 7.0 %collective-permute-start.13 = (bf16[512,128]{1,0:T(8,128)(2,1)S(1)}, bf16[512,128]{1,0:T(8,128)(2,1)S(1)}, u32[]{:S(2)}, u32[]{:S(2)}) collective-permute-start(bf16[512,128]{1,0:T(8,128)(2,1)S(1)} %project.7.refs_0_), channel_id=1, source_target_pairs={{0,2},{1,3},{2,0},{3,1},{4,6},{5,7},{6,4},{7,5},{8,10},{9,11},{10,... | collective-permute-start | bytes 393224 | tf_op jit(solution)/shard_map/ppermute | solution.py:20
  51.6 5.5 %collective-permute-start.14 = (bf16[512,128]{1,0:T(8,128)(2,1)S(1)}, bf16[512,128]{1,0:T(8,128)(2,1)S(1)}, u32[]{:S(2)}, u32[]{:S(2)}) collective-permute-start(bf16[512,128]{1,0:T(8,128)(2,1)S(1)} %project.7.refs_0_), channel_id=1, source_target_pairs={{0,4},{1,5},{2,6},{3,7},{4,0},{5,1},{6,2},{7,3},{8,12},{9,13},{10,... | collective-permute-start | bytes 393224 | tf_op jit(solution)/shard_map/ppermute | solution.py:20
  53.1 5.9 %collective-permute-start.15 = (bf16[512,128]{1,0:T(8,128)(2,1)S(1)}, bf16[512,128]{1,0:T(8,128)(2,1)S(1)}, u32[]{:S(2)}, u32[]{:S(2)}) collective-permute-start(bf16[512,128]{1,0:T(8,128)(2,1)S(1)} %project.7.refs_0_), channel_id=1, source_target_pairs={{0,6},{1,7},{2,4},{3,5},{4,2},{5,3},{6,0},{7,1},{8,14},{9,15},{10,... | collective-permute-start | bytes 393224 | tf_op jit(solution)/shard_map/ppermute | solution.py:20
  53.6 12.5 %collective-permute-start.20 = (bf16[1024,128]{1,0:T(8,128)(2,1)S(1)}, bf16[1024,128]{1,0:T(8,128)(2,1)S(1)}, u32[]{:S(2)}, u32[]{:S(2)}) collective-permute-start(bf16[1024,128]{1,0:T(8,128)(2,1)S(1)} %regroup.24.refs_0_), channel_id=1, source_target_pairs={{0,16},{8,24},{16,0},{24,8},{1,17},{9,25},{17,1},{25,9},{2,18},{10... | collective-permute-start | bytes 786440 | tf_op jit(solution)/shard_map/ppermute | solution.py:25
  59.0 7.7 %collective-permute-start.16 = (bf16[2048,128]{1,0:T(8,128)(2,1)S(1)}, bf16[2048,128]{1,0:T(8,128)(2,1)S(1)}, u32[]{:S(2)}, u32[]{:S(2)}) collective-permute-start(bf16[2048,128]{1,0:T(8,128)(2,1)S(1)} %regroup.21.held), channel_id=1, source_target_pairs={{0,1},{1,0},{2,3},{3,2},{4,5},{5,4},{6,7},{7,6},{8,9},{9,8},{10,11... | collective-permute-start | bytes 1572872 | tf_op jit(solution)/shard_map/ppermute | solution.py:20
  59.1 20.1 %collective-permute-start.18 = (bf16[1536,256]{1,0:T(8,128)(2,1)S(1)}, bf16[1536,256]{1,0:T(8,128)(2,1)S(1)}, u32[]{:S(2)}, u32[]{:S(2)}) collective-permute-start(bf16[1536,256]{1,0:T(8,128)(2,1)S(1)} %regroup.23.refs_0_), channel_id=1, source_target_pairs={{0,2},{1,3},{2,0},{3,1},{4,6},{5,7},{6,4},{7,5},{8,10},{9,11},{10,... | collective-permute-start | bytes 2359304 | tf_op jit(solution)/shard_map/ppermute | solution.py:20
  59.7 19.7 %collective-permute-start.19 = (bf16[1536,256]{1,0:T(8,128)(2,1)S(1)}, bf16[1536,256]{1,0:T(8,128)(2,1)S(1)}, u32[]{:S(2)}, u32[]{:S(2)}) collective-permute-start(bf16[1536,256]{1,0:T(8,128)(2,1)S(1)} %regroup.23.refs_0_), channel_id=1, source_target_pairs={{0,4},{1,5},{2,6},{3,7},{4,0},{5,1},{6,2},{7,3},{8,12},{9,13},{10,... | collective-permute-start | bytes 2359304 | tf_op jit(solution)/shard_map/ppermute | solution.py:20
  66.1 13.1 %collective-permute-start.21 = (bf16[2048,128]{1,0:T(8,128)(2,1)S(1)}, bf16[2048,128]{1,0:T(8,128)(2,1)S(1)}, u32[]{:S(2)}, u32[]{:S(2)}) collective-permute-start(bf16[2048,128]{1,0:T(8,128)(2,1)S(1)} %regroup.25), channel_id=1, source_target_pairs={{0,8},{8,0},{16,24},{24,16},{1,9},{9,1},{17,25},{25,17},{2,10},{10... | collective-permute-start | bytes 1572872 | tf_op jit(solution)/shard_map/ppermute | solution.py:25
  79.5 12.1 %collective-permute-start.22 = (bf16[768,256]{1,0:T(8,128)(2,1)S(1)}, bf16[768,256]{1,0:T(8,128)(2,1)S(1)}, u32[]{:S(2)}, u32[]{:S(2)}) collective-permute-start(bf16[768,256]{1,0:T(8,128)(2,1)S(1)} %get-tuple-element.87), channel_id=1, source_target_pairs={{0,4},{1,5},{2,6},{3,7},{4,0},{5,1},{6,2},{7,3},{8,12},{9,13},{10,... | collective-permute-start | bytes 1179656 | tf_op jit(solution)/shard_map/ppermute | solution.py:20
  80.1 12.1 %collective-permute-start.23 = (bf16[768,256]{1,0:T(8,128)(2,1)S(1)}, bf16[768,256]{1,0:T(8,128)(2,1)S(1)}, u32[]{:S(2)}, u32[]{:S(2)}) collective-permute-start(bf16[768,256]{1,0:T(8,128)(2,1)S(1)} %get-tuple-element.88), channel_id=1, source_target_pairs={{0,2},{1,3},{2,0},{3,1},{4,6},{5,7},{6,4},{7,5},{8,10},{9,11},{10,... | collective-permute-start | bytes 1179656 | tf_op jit(solution)/shard_map/ppermute | solution.py:20
  81.6 18.4 %collective-permute-start.24 = (bf16[1536,128]{1,0:T(8,128)(2,1)S(1)}, bf16[1536,128]{1,0:T(8,128)(2,1)S(1)}, u32[]{:S(2)}, u32[]{:S(2)}) collective-permute-start(bf16[1536,128]{1,0:T(8,128)(2,1)S(1)} %get-tuple-element.82.refs_0_), channel_id=1, source_target_pairs={{0,4},{1,5},{2,6},{3,7},{4,0},{5,1},{6,2},{7,3},{8,12},{9,13},{10,... | collective-permute-start | bytes 1179656 | tf_op jit(solution)/shard_map/ppermute | solution.py:20
  83.2 17.4 %collective-permute-start.25 = (bf16[1536,128]{1,0:T(8,128)(2,1)S(1)}, bf16[1536,128]{1,0:T(8,128)(2,1)S(1)}, u32[]{:S(2)}, u32[]{:S(2)}) collective-permute-start(bf16[1536,128]{1,0:T(8,128)(2,1)S(1)} %get-tuple-element.83.refs_1_), channel_id=1, source_target_pairs={{0,2},{1,3},{2,0},{3,1},{4,6},{5,7},{6,4},{7,5},{8,10},{9,11},{10,... | collective-permute-start | bytes 1179656 | tf_op jit(solution)/shard_map/ppermute | solution.py:20
  92.7 13.5 %collective-permute-start.26 = (bf16[512,256]{1,0:T(8,128)(2,1)S(1)}, bf16[512,256]{1,0:T(8,128)(2,1)S(1)}, u32[]{:S(2)}, u32[]{:S(2)}) collective-permute-start(bf16[512,256]{1,0:T(8,128)(2,1)S(1)} %project.10.refs_0_), channel_id=1, source_target_pairs={{0,2},{1,3},{2,0},{3,1},{4,6},{5,7},{6,4},{7,5},{8,10},{9,11},{10,... | collective-permute-start | bytes 786440 | tf_op jit(solution)/shard_map/ppermute | solution.py:20
  94.2 12.0 %collective-permute-start.27 = (bf16[512,256]{1,0:T(8,128)(2,1)S(1)}, bf16[512,256]{1,0:T(8,128)(2,1)S(1)}, u32[]{:S(2)}, u32[]{:S(2)}) collective-permute-start(bf16[512,256]{1,0:T(8,128)(2,1)S(1)} %project.10.refs_0_), channel_id=1, source_target_pairs={{0,4},{1,5},{2,6},{3,7},{4,0},{5,1},{6,2},{7,3},{8,12},{9,13},{10,... | collective-permute-start | bytes 786440 | tf_op jit(solution)/shard_map/ppermute | solution.py:20
  95.7 15.1 %collective-permute-start.28 = (bf16[512,256]{1,0:T(8,128)(2,1)S(1)}, bf16[512,256]{1,0:T(8,128)(2,1)S(1)}, u32[]{:S(2)}, u32[]{:S(2)}) collective-permute-start(bf16[512,256]{1,0:T(8,128)(2,1)S(1)} %project.10.refs_0_), channel_id=1, source_target_pairs={{0,6},{1,7},{2,4},{3,5},{4,2},{5,3},{6,0},{7,1},{8,14},{9,15},{10,... | collective-permute-start | bytes 786440 | tf_op jit(solution)/shard_map/ppermute | solution.py:20
  111.0 10.5 %collective-permute-start.30 = (bf16[512,128]{1,0:T(8,128)(2,1)S(1)}, bf16[512,128]{1,0:T(8,128)(2,1)S(1)}, u32[]{:S(2)}, u32[]{:S(2)}) collective-permute-start(bf16[512,128]{1,0:T(8,128)(2,1)S(1)} %project.11.refs_0_), channel_id=1, source_target_pairs={{0,2},{1,3},{2,0},{3,1},{4,6},{5,7},{6,4},{7,5},{8,10},{9,11},{10,... | collective-permute-start | bytes 393224 | tf_op jit(solution)/shard_map/ppermute | solution.py:20
  112.5 9.0 %collective-permute-start.31 = (bf16[512,128]{1,0:T(8,128)(2,1)S(1)}, bf16[512,128]{1,0:T(8,128)(2,1)S(1)}, u32[]{:S(2)}, u32[]{:S(2)}) collective-permute-start(bf16[512,128]{1,0:T(8,128)(2,1)S(1)} %project.11.refs_0_), channel_id=1, source_target_pairs={{0,4},{1,5},{2,6},{3,7},{4,0},{5,1},{6,2},{7,3},{8,12},{9,13},{10,... | collective-permute-start | bytes 393224 | tf_op jit(solution)/shard_map/ppermute | solution.py:20
  113.0 8.5 %collective-permute-start.32 = (bf16[512,128]{1,0:T(8,128)(2,1)S(1)}, bf16[512,128]{1,0:T(8,128)(2,1)S(1)}, u32[]{:S(2)}, u32[]{:S(2)}) collective-permute-start(bf16[512,128]{1,0:T(8,128)(2,1)S(1)} %project.11.refs_0_), channel_id=1, source_target_pairs={{0,6},{1,7},{2,4},{3,5},{4,2},{5,3},{6,0},{7,1},{8,14},{9,15},{10,... | collective-permute-start | bytes 393224 | tf_op jit(solution)/shard_map/ppermute | solution.py:20
  121.6 7.2 %collective-permute-start.33 = (bf16[2048,128]{1,0:T(8,128)(2,1)S(1)}, bf16[2048,128]{1,0:T(8,128)(2,1)S(1)}, u32[]{:S(2)}, u32[]{:S(2)}) collective-permute-start(bf16[2048,128]{1,0:T(8,128)(2,1)S(1)} %regroup.29.held), channel_id=1, source_target_pairs={{0,1},{1,0},{2,3},{3,2},{4,5},{5,4},{6,7},{7,6},{8,9},{9,8},{10,11... | collective-permute-start | bytes 1572872 | tf_op jit(solution)/shard_map/ppermute | solution.py:20
  (6 other events, 39.6 us)
